TPU v7x, 32 devices: a whole 2x2x4 slice. The times are simulated.
32 devices in a mesh: section: 2 (over x), seq: 2 (over core), dp: 8 (over z, y).
Axes of the slice: x: 2, y: 2, z: 4, core: 2. Of those that a mesh axis runs over, the one named last changes fastest.
Arguments:
- tokens: bfloat16 [2, 8, 1024, 768], P(None, 'dp', 'seq'), may hold values from -6 to 6
- cotangent: bfloat16 [2, 8, 1024, 768], P(None, 'dp', 'seq'), may hold values from -6 to 6
- segments: int32 [2, 8, 1024], P(None, 'dp', 'seq'), may hold values from 0 to 2, as said below
- norm_gain: bfloat16 [2, 768], P('section', ('seq', 'dp')), may hold values from 0.099609375 to 1.8984375
- in_weight: bfloat16 [2, 768, 3352], P('section', ('seq', 'dp')), may hold values from -0.21875 to 0.21875
- conv_weight: bfloat16 [2, 4, 1792], P('section', None, ('seq', 'dp')), may hold values from -3 to 3
- conv_bias: bfloat16 [2, 1792], P('section', ('seq', 'dp')), may hold values from -3 to 3
- dt_bias: float32 [2, 24], P('section'), may hold values from -6.9 to -2.3
- decay_log: float32 [2, 24], P('section'), may hold values from 0 to 2.77
- skip_gain: float32 [2, 24], P('section'), may hold values from 0.5 to 1.5
- out_gain: bfloat16 [2, 1536], P('section', ('seq', 'dp')), may hold values from 0.099609375 to 1.8984375
- out_weight: bfloat16 [2, 1536, 768], P('section', ('seq', 'dp')), may hold values from -0.15625 to 0.15625
Outputs:
- section_outputs: bfloat16 [2, 2, 8, 1024, 768], P('section', None, 'dp', 'seq')
- input_grads: float32 [2, 2, 8, 1024, 768], P('section', None, 'dp', 'seq')
- grad_norm_gain: float32 [2, 768], P('section', ('seq', 'dp'))
- grad_in_weight: float32 [2, 768, 3352], P('section', ('seq', 'dp'))
- grad_conv_weight: float32 [2, 4, 1792], P('section', None, ('seq', 'dp'))
- grad_conv_bias: float32 [2, 1792], P('section', ('seq', 'dp'))
- grad_dt_bias: float32 [2, 24], P('section')
- grad_decay_log: float32 [2, 24], P('section')
- grad_skip_gain: float32 [2, 24], P('section')
- grad_out_gain: float32 [2, 1536], P('section', ('seq', 'dp'))
- grad_out_weight: float32 [2, 1536, 768], P('section', ('seq', 'dp'))
Inputs may be any that keep to these rules, and one draw needn't show every extreme that they name: `segments`: each sequence's document numbers start at 0 and never fall along it; tokens with equal numbers form one document.
All inputs are finite; a program needn't handle non-finite values.
Results may differ from a plain program's by a relative error of at most 0.012.
Values may be sent and summed in bfloat16 or wider, within the bound.
No kernel may reach another device: no remote copies, remote signals or barrier semaphores. Data moves between devices by JAX's collectives and lax.ppermute only.
A program may use at most 384 MiB of HBM per device.

v0:
```python
from functools import partial

import jax
import jax.numpy as jnp
from jax import lax
from jax.sharding import PartitionSpec as P

DI = 1536
N = 128
XC = 1792


epsilon = 1e-05
highest = lax.Precision.HIGHEST


def shifted(value, axis, steps):
    count = lax.axis_size(axis)
    initial, last = (max(0, -steps), min(count, count - steps))
    return lax.ppermute(value, axis, [(source, source + steps) for source in range(initial, last)])


def rms_scale(values, gain_vector):
    return values * lax.rsqrt(jnp.mean(values * values, -1, keepdims=True) + epsilon) * gain_vector


def conv_part(
    conv_in, dt_raw, rim_rows, conv_weight, conv_bias, dt_bias, decay_log, seg_ids, rim_ids
):
    pieces = conv_in.shape[1]
    padded = jnp.concatenate([rim_rows, conv_in], 1)
    seg_pad = jnp.concatenate([rim_ids, seg_ids], 1)
    conv_out = conv_bias + jnp.zeros_like(conv_in)
    for offset in range(conv_weight.shape[0]):
        doc_match = (seg_pad[:, offset : offset + pieces] == seg_ids).astype(jnp.float32)
        conv_out = (
            conv_out
            + conv_weight[offset] * padded[:, offset : offset + pieces] * doc_match[..., None]
        )
    activated = jax.nn.silu(conv_out)
    step_size = jax.nn.softplus(dt_raw + dt_bias)
    log_decay = -jnp.exp(decay_log) * step_size
    return (
        activated[..., :DI],
        activated[..., DI : DI + N],
        activated[..., DI + N :],
        step_size,
        log_decay,
    )


def state_part(x_in, b_in, step_size, log_decay, seg_ids, rim_ids):
    batch_size, pieces, head_count = step_size.shape
    cum_decay = jnp.cumsum(log_decay, 1)
    last_decay = cum_decay[:, -1]
    tail_match = (seg_ids == seg_ids[:, -1:]).astype(jnp.float32)
    tail_weight = jnp.exp(last_decay[:, None, :] - cum_decay) * tail_match[..., None] * step_size
    heads_x = x_in.reshape(batch_size, pieces, head_count, -1)
    local_state = jnp.einsum("bsh,bshp,bsn->bhpn", tail_weight, heads_x, b_in, precision=highest)
    through = jnp.exp(last_decay) * (seg_ids[:, -1:] == rim_ids[:, -1:]).astype(jnp.float32)
    return (through, local_state)


def out_part(
    x_in, b_in, c_in, step_size, log_decay, gate_z, skip_gain, out_gain, incoming, seg_ids, rim_ids
):
    batch_size, pieces, head_count = step_size.shape
    cum_decay = jnp.cumsum(log_decay, 1)
    cum_heads = jnp.swapaxes(cum_decay, 1, 2)
    step_heads = jnp.swapaxes(step_size, 1, 2)
    positions = jnp.arange(pieces)
    causal = positions[:, None] >= positions[None, :]
    same_doc = ((seg_ids[:, :, None] == seg_ids[:, None, :]) & causal).astype(jnp.float32)[:, None]
    decay_gap = cum_heads[:, :, :, None] - cum_heads[:, :, None, :]
    kernel = jnp.exp(jnp.where(same_doc > 0, decay_gap, 0.0)) * same_doc
    scores = jnp.einsum("btn,bsn->bts", c_in, b_in, precision=highest)
    mixing = scores[:, None] * kernel * step_heads[:, :, None, :]
    heads_x = x_in.reshape(batch_size, pieces, head_count, -1)
    result = jnp.einsum("bhts,bshp->bthp", mixing, heads_x, precision=highest)
    carry_in = jnp.exp(cum_decay) * (seg_ids == rim_ids[:, -1:]).astype(jnp.float32)[..., None]
    result = result + carry_in[..., None] * jnp.einsum(
        "bhpn,btn->bthp", incoming, c_in, precision=highest
    )
    result = result + skip_gain[:, None] * heads_x
    gated_out = result.reshape(batch_size, pieces, -1) * jax.nn.silu(gate_z)
    return rms_scale(gated_out, out_gain)


def pass_forward(through, local_state):

    def relay_step(turn_index, incoming):
        return shifted(through[..., None, None] * incoming + local_state, "seq", 1)

    return lax.fori_loop(0, lax.axis_size("seq") - 1, relay_step, jnp.zeros_like(local_state))


def pass_backward(through, local_grad):

    def relay_back(turn_index, outgoing):
        return shifted(through[..., None, None] * outgoing + local_grad, "seq", -1)

    return lax.fori_loop(0, lax.axis_size("seq") - 1, relay_back, jnp.zeros_like(local_grad))


def unpack(gathered):
    return (
        gathered[0][0].astype(jnp.float32),
        gathered[1][0],
        gathered[2][0].astype(jnp.float32),
        gathered[3][0].astype(jnp.float32),
        gathered[4][0].astype(jnp.float32),
        gathered[5][0],
    )


def forward_tick(source, seg_ids, weights, head_params):
    norm_gain, in_weight, conv_weight, conv_bias, out_gain, out_weight = weights
    dt_bias, decay_log, skip_gain = head_params
    normed = rms_scale(source, norm_gain).astype(jnp.bfloat16)
    projected = jnp.einsum("bld,dk->blk", normed, in_weight, preferred_element_type=jnp.float32)
    rim_count = conv_weight.shape[0] - 1
    conv_in = projected[..., DI : DI + XC]
    rim_rows, rim_ids = shifted((conv_in[:, -rim_count:], seg_ids[:, -rim_count:]), "seq", 1)
    x_in, b_in, c_in, step_size, log_decay = conv_part(
        conv_in,
        projected[..., DI + XC :],
        rim_rows,
        conv_weight,
        conv_bias,
        dt_bias,
        decay_log,
        seg_ids,
        rim_ids,
    )
    through, local_state = state_part(x_in, b_in, step_size, log_decay, seg_ids, rim_ids)
    incoming = pass_forward(through, local_state)
    normed_out = out_part(
        x_in,
        b_in,
        c_in,
        step_size,
        log_decay,
        projected[..., :DI],
        skip_gain,
        out_gain,
        incoming,
        seg_ids,
        rim_ids,
    ).astype(jnp.bfloat16)
    result = source + jnp.einsum(
        "blk,kd->bld", normed_out, out_weight, preferred_element_type=jnp.float32
    )
    return (result, (rim_rows, rim_ids, incoming))


def backward_tick(source, seg_ids, kept_items, grad_out, weights, head_params):
    norm_gain, in_weight, conv_weight, conv_bias, out_gain, out_weight = weights
    dt_bias, decay_log, skip_gain = head_params
    rim_rows, rim_ids, incoming = kept_items
    normed_float, norm_pull = jax.vjp(rms_scale, source, norm_gain)
    normed = normed_float.astype(jnp.bfloat16)
    projected = jnp.einsum("bld,dk->blk", normed, in_weight, preferred_element_type=jnp.float32)
    conv_fn = partial(conv_part, seg_ids=seg_ids, rim_ids=rim_ids)
    conv_values, conv_pull = jax.vjp(
        conv_fn,
        projected[..., DI : DI + XC],
        projected[..., DI + XC :],
        rim_rows,
        conv_weight,
        conv_bias,
        dt_bias,
        decay_log,
    )
    x_in, b_in, c_in, step_size, log_decay = conv_values
    state_fn = partial(state_part, seg_ids=seg_ids, rim_ids=rim_ids)
    state_values, state_pull = jax.vjp(state_fn, x_in, b_in, step_size, log_decay)
    out_fn = partial(out_part, seg_ids=seg_ids, rim_ids=rim_ids)
    out_float, out_pull = jax.vjp(
        out_fn,
        x_in,
        b_in,
        c_in,
        step_size,
        log_decay,
        projected[..., :DI],
        skip_gain,
        out_gain,
        incoming,
    )
    normed_out = out_float.astype(jnp.bfloat16)
    grad_low = grad_out.astype(jnp.bfloat16)
    grad_normed_out = jnp.einsum(
        "bld,kd->blk", grad_low, out_weight, preferred_element_type=jnp.float32
    )
    out_grads = out_pull(grad_normed_out)
    state_grad = pass_backward(state_values[0], out_grads[8])
    grad_through = jnp.sum(state_grad * incoming, axis=(2, 3))
    state_grads = state_pull((grad_through, state_grad))
    conv_grads = conv_pull(
        (
            out_grads[0] + state_grads[0],
            out_grads[1] + state_grads[1],
            out_grads[2],
            out_grads[3] + state_grads[2],
            out_grads[4] + state_grads[3],
        )
    )
    returned = shifted(conv_grads[2], "seq", -1)
    pieces = source.shape[1]
    grad_conv_in = conv_grads[0] + jnp.pad(
        returned, ((0, 0), (pieces - returned.shape[1], 0), (0, 0))
    )
    grad_proj = jnp.concatenate([out_grads[5], grad_conv_in, conv_grads[1]], -1).astype(
        jnp.bfloat16
    )
    grad_normed = jnp.einsum(
        "blk,dk->bld", grad_proj, in_weight, preferred_element_type=jnp.float32
    )
    grad_source, grad_norm_gain = norm_pull(grad_normed)
    products = (normed, grad_proj, normed_out, grad_low)
    small_grads = (
        grad_norm_gain,
        conv_grads[3],
        conv_grads[4],
        out_grads[7],
        conv_grads[5],
        conv_grads[6],
        out_grads[6],
    )
    return (grad_out + grad_source, products, small_grads)


def shards(
    tokens,
    cotangent,
    segments,
    norm_gain,
    in_weight,
    conv_weight,
    conv_bias,
    dt_bias,
    decay_log,
    skip_gain,
    out_gain,
    out_weight,
):
    is_first = lax.axis_index("section") == 0
    micro_count = tokens.shape[0]
    packed = (norm_gain, in_weight, conv_weight, conv_bias, out_gain, out_weight)
    weights = unpack(
        (
            lax.all_gather(packed[0], ("seq", "dp"), axis=1, tiled=True),
            lax.all_gather(packed[1], ("seq", "dp"), axis=1, tiled=True),
            lax.all_gather(packed[2], ("seq", "dp"), axis=2, tiled=True),
            lax.all_gather(packed[3], ("seq", "dp"), axis=1, tiled=True),
            lax.all_gather(packed[4], ("seq", "dp"), axis=1, tiled=True),
            lax.all_gather(packed[5], ("seq", "dp"), axis=1, tiled=True),
        )
    )
    head_params = (dt_bias[0], decay_log[0], skip_gain[0])
    seg_float = segments.astype(jnp.float32)
    received = jnp.zeros(tokens.shape[1:], jnp.float32)
    records = []
    for tick_index in range(micro_count + 1):
        early_index = min(tick_index, micro_count - 1)
        late_index = max(tick_index - 1, 0)
        source = jnp.where(is_first, tokens[early_index].astype(jnp.float32), received)
        seg_ids = jnp.where(is_first, seg_float[early_index], seg_float[late_index])
        result, kept_items = forward_tick(source, seg_ids, weights, head_params)
        sent_out = result.astype(jnp.bfloat16)
        if tick_index < micro_count:
            received = shifted(sent_out, "section", 1).astype(jnp.float32)
        records.append((source, seg_ids, kept_items, sent_out))
    section_outputs = jnp.stack(
        [
            jnp.where(is_first, records[index_mb][3], records[index_mb + 1][3])
            for index_mb in range(micro_count)
        ]
    )[None]
    backward_weights = unpack(
        (
            lax.all_gather(packed[0], ("seq", "dp"), axis=1, tiled=True),
            lax.all_gather(packed[1], ("seq", "dp"), axis=1, tiled=True),
            lax.all_gather(packed[2], ("seq", "dp"), axis=2, tiled=True),
            lax.all_gather(packed[3], ("seq", "dp"), axis=1, tiled=True),
            lax.all_gather(packed[4], ("seq", "dp"), axis=1, tiled=True),
            lax.all_gather(packed[5], ("seq", "dp"), axis=1, tiled=True),
        )
    )
    pick_section = partial(jnp.where, is_first)
    received_grad = jnp.zeros(tokens.shape[1:], jnp.float32)
    product_list = []
    input_rows = []
    small_total = None
    for tick_index in range(micro_count + 1):
        chosen = jax.tree.map(
            pick_section, records[max(tick_index - 1, 0)], records[min(tick_index + 1, micro_count)]
        )
        valid_first = 1.0 if tick_index >= 1 else 0.0
        valid_second = 1.0 if tick_index < micro_count else 0.0
        valid_mask = jnp.where(is_first, valid_first, valid_second)
        own_grad = cotangent[min(tick_index, micro_count - 1)].astype(jnp.float32)
        grad_out = jnp.where(is_first, received_grad, own_grad) * valid_mask
        grad_source, tick_products, tick_small = backward_tick(
            chosen[0], chosen[1], chosen[2], grad_out, backward_weights, head_params
        )
        grad_sent = grad_source.astype(jnp.bfloat16)
        if tick_index < micro_count:
            received_grad = shifted(grad_sent, "section", -1).astype(jnp.float32)
        input_rows.append(jnp.where(is_first, grad_source, grad_sent.astype(jnp.float32)))
        product_list.append(tick_products)
        small_total = (
            tick_small if small_total is None else jax.tree.map(jnp.add, small_total, tick_small)
        )
    input_grads = jnp.stack(
        [
            jnp.where(is_first, input_rows[index_mb + 1], input_rows[index_mb])
            for index_mb in range(micro_count)
        ]
    )[None]

    def stacked_rows(position):
        return jnp.concatenate(
            [entry[position].reshape(-1, entry[position].shape[-1]) for entry in product_list], 0
        )

    grad_in_weight = jnp.einsum(
        "rd,rk->dk", stacked_rows(0), stacked_rows(1), preferred_element_type=jnp.float32
    )
    grad_out_weight = jnp.einsum(
        "rk,rd->kd", stacked_rows(2), stacked_rows(3), preferred_element_type=jnp.float32
    )
    (
        grad_norm_gain,
        grad_conv_weight,
        grad_conv_bias,
        grad_out_gain,
        grad_dt_bias,
        grad_decay_log,
        grad_skip_gain,
    ) = small_total
    conv_turned = jnp.swapaxes(grad_conv_weight, 0, 1)
    summed = (
        lax.psum_scatter(grad_norm_gain[None], ("seq", "dp"), scatter_dimension=1, tiled=True),
        lax.psum_scatter(grad_in_weight[None], ("seq", "dp"), scatter_dimension=1, tiled=True),
        lax.psum_scatter(conv_turned[None], ("seq", "dp"), scatter_dimension=1, tiled=True),
        lax.psum_scatter(grad_conv_bias[None], ("seq", "dp"), scatter_dimension=1, tiled=True),
        lax.psum_scatter(grad_out_gain[None], ("seq", "dp"), scatter_dimension=1, tiled=True),
        lax.psum_scatter(grad_out_weight[None], ("seq", "dp"), scatter_dimension=1, tiled=True),
    )
    head_sums = lax.psum(
        (grad_dt_bias[None], grad_decay_log[None], grad_skip_gain[None]), ("seq", "dp")
    )
    conv_summed = jnp.swapaxes(summed[2], 1, 2)
    return (
        section_outputs,
        input_grads,
        summed[0],
        summed[1],
        conv_summed,
        summed[3],
        head_sums[0],
        head_sums[1],
        head_sums[2],
        summed[4],
        summed[5],
    )


def solution(mesh):
    placed = (
        P(None, "dp", "seq", None),
        P(None, "dp", "seq", None),
        P(None, "dp", "seq"),
        P("section", ("seq", "dp")),
        P("section", ("seq", "dp"), None),
        P("section", None, ("seq", "dp")),
        P("section", ("seq", "dp")),
        P("section", None),
        P("section", None),
        P("section", None),
        P("section", ("seq", "dp")),
        P("section", ("seq", "dp"), None),
    )
    return jax.shard_map(
        shards,
        mesh=mesh,
        in_specs=placed,
        out_specs=(
            P("section", None, "dp", "seq", None),
            P("section", None, "dp", "seq", None),
            P("section", ("seq", "dp")),
            P("section", ("seq", "dp"), None),
            P("section", None, ("seq", "dp")),
            P("section", ("seq", "dp")),
            P("section", None),
            P("section", None),
            P("section", None),
            P("section", ("seq", "dp")),
            P("section", ("seq", "dp"), None),
        ),
        check_vma=False,
    )
```

profile of v0, /device:TPU:0, one launch (start us, length us, event | category | flops | bytes accessed | tf_op | source)
XLA Modules:
  0.0 1711.2 jit_solution(16316307560731002819)
XLA Ops:
  22.2 62.7 %all-reduce.44 = (bf16[1536]{0:T(1024)(128)(2,1)S(1)}, bf16[768]{0:T(1024)(128)(2,1)S(1)}, bf16[1792]{0:T(1024)(128)(2,1)S(1)}) all-reduce(bf16[1536]{0:T(1024)(128)(2,1)S(1)} %dynamic-update-slice.2, bf16[768]{0:T(1024)(128)(2,1)S(1)} %dynamic-update-slice.1, ...), channel_id=1, replica_groups=mesh['section'=2,'seq'=2,'dp'=8] {'seq','dp'}, use_global_device_ids=true, to_apply=%add.41 | all-reduce | flops 4096 | bytes 16384
  88.3 40.0 %all_gather.25 = bf16[1,4,1792]{1,0,2:T(2,128)(2,1)S(1)} all-gather(bf16[1,4,112]{1,0,2:T(2,128)(2,1)S(1)} %copy.744), channel_id=1, replica_groups=mesh['section'=2,'seq'=2,'dp'=8] {'seq','dp'}, dimensions={2}, use_global_device_ids=true | all-gather | bytes 15232 | tf_op jit(solution)/shard_map/all_gather | solution.py:254
  129.3 37.1 %slice_reduce_fusion.3 = (f32[1792]{0:T(1024)S(1)}, f32[1792]{0:T(1024)S(1)}, f32[1792]{0:T(1024)S(1)}, f32[1792]{0:T(1024)S(1)}) fusion(f32[1,4,1792]{1,0,2:T(1,128)S(1)} %convert_element_type.497), kind=kLoop, calls=%fused_computation.533 | loop fusion | bytes 57344 | tf_op jit(solution)/shard_map/slice | solution.py:38
  203.9 9.5 divide_multiply_fusion.2
  226.7 28.2 %fusion.35 = f32[24,64,512]{2,1,0:T(8,128)S(1)} fusion(f32[512,24,64]{0,2,1:T(8,128)S(1)} %bitcast.1279, f32[24,512]{1,0:T(8,128)S(1)} %copy-done.211, f32[512,512]{1,0:T(8,128)S(1)} %copy-done.118, f32[24,512]{1,0:T(8,128)S(1)} %copy-done.224, f32[512,512]{1,0:T(8,128)S(1)} %fusion.545, pred[512,512]{1,0:T(8,128)(4,1)S(1)} %get-tuple-element.417), kind=kOutput, calls=%fused_computation.41 | convolution fusion | flops 4863295488 | bytes 8749056 | tf_op jit(solution)/shard_map/bhts,bshp->bthp/dot_general | solution.py:79
  311.4 9.5 divide_multiply_fusion.1
  333.3 28.0 %fusion.28 = f32[24,64,512]{2,1,0:T(8,128)S(1)} fusion(f32[512,24,64]{0,2,1:T(8,128)S(1)} %bitcast.1282, f32[24,512]{1,0:T(8,128)S(1)} %copy-done.212, f32[512,512]{1,0:T(8,128)S(1)} %copy-done.119, f32[24,512]{1,0:T(8,128)S(1)} %copy-done.225, f32[512,512]{1,0:T(8,128)S(1)} %copy-done.134, pred[512,512]{1,0:T(8,128)(4,1)S(1)} %get-tuple-element.380), kind=kOutput, calls=%fused_computation.34 | convolution fusion | flops 4863295488 | bytes 8749056 | tf_op jit(solution)/shard_map/bhts,bshp->bthp/dot_general | solution.py:79
  390.6 8.4 collective-permute-done.7
  483.5 9.5 divide_multiply_fusion
  543.5 31.2 %fusion.233 = f32[1,512,24,64]{1,3,2,0:T(8,128)} fusion(f32[1,512,24,64]{1,3,2,0:T(8,128)S(1)} %bitcast.1265, f32[512,24,64]{0,2,1:T(8,128)S(1)} %fusion.455, f32[512,24,64]{0,2,1:T(8,128)S(1)} %bitcast.1264, f32[24,512]{1,0:T(8,128)S(1)} %copy-done.209, f32[512,512]{1,0:T(8,128)S(1)} %copy-done.116, f32[24,512]{1,0:T(8,128)S(1)} %copy-done.222, ...), kind=kOutput, calls=%fused_computation.314 | convolution fusion | flops 4866441216 | bytes 15089760 | tf_op jit(solution)/shard_map/jvp(bhts,bshp->bthp)/dot_general | solution.py:79
  605.6 40.1 %fusion.43 = (f32[24,512]{1,0:T(8,128)}, f32[24,512]{1,0:T(8,128)}, f32[24,512]{1,0:T(8,128)}, f32[512,512]{1,0:T(8,128)}) fusion(f32[24,512]{1,0:T(8,128)S(1)} %copy-done.209, f32[512,512]{1,0:T(8,128)S(1)} %copy-done.117, f32[24,512]{1,0:T(8,128)S(1)} %copy-done.222, f32[512,512]{1,0:T(8,128)} %copy-done.132, pred[512,512]{1,0:T(8,128)(4,1)S(1)} %copy-done.176, ...), kind=kOutput, calls=%fused_computation.49 | convolution fusion | flops 4925911040 | bytes 9945088 | tf_op jit(solution)/shard_map/transpose(jvp(bhts,bshp->bthp))/dot_general | solution.py:79
  647.0 24.8 %bitcast_add_fusion.4 = f32[1,512,24,64]{1,3,2,0:T(8,128)} fusion(f32[1,512,24,64]{1,3,2,0:T(8,128)S(1)} %bitcast.1287, f32[24,64,512]{2,1,0:T(8,128)S(1)} %bitcast.1286, f32[24,512]{1,0:T(8,128)S(1)} %copy-done.210, f32[512,512]{1,0:T(8,128)S(1)} %copy-done.117, f32[24,512]{1,0:T(8,128)S(1)} %copy-done.223, f32[512,512]{1,0:T(8,128)S(1)} %copy-done.133, ...), kind=kOutput, calls=%fused_computation.312 | convolution fusion | flops 4864868352 | bytes 11894880 | tf_op jit(solution)/shard_map/transpose(jvp(bhts,bshp->bthp))/dot_general | solution.py:79
  675.7 30.9 %fusion.232 = f32[1,512,24,64]{1,3,2,0:T(8,128)} fusion(f32[1,512,24,64]{1,3,2,0:T(8,128)S(1)} %bitcast.1260, f32[512,24,64]{0,2,1:T(8,128)S(1)} %fusion.449, f32[512,24,64]{0,2,1:T(8,128)S(1)} %bitcast.1259, f32[24,512]{1,0:T(8,128)S(1)} %copy-done.208, f32[512,512]{1,0:T(8,128)S(1)} %copy-done.137, f32[24,512]{1,0:T(8,128)S(1)} %copy-done.220, ...), kind=kOutput, calls=%fused_computation.311 | convolution fusion | flops 4866441216 | bytes 15089760 | tf_op jit(solution)/shard_map/jvp(bhts,bshp->bthp)/dot_general | solution.py:79
  761.6 7.5 fusion.623
  769.1 8.9 multiply_multiply_fusion.11
  820.2 7.0 fusion.313
  830.7 31.0 %fusion.231 = f32[1,512,24,64]{1,3,2,0:T(8,128)} fusion(f32[1,512,24,64]{1,3,2,0:T(8,128)S(1)} %bitcast.1255, f32[512,24,64]{0,2,1:T(8,128)S(1)} %copy-done.53, f32[512,24,64]{0,2,1:T(8,128)S(1)} %bitcast.1254, f32[24,512]{1,0:T(8,128)S(1)} %copy-done.205, f32[512,512]{1,0:T(8,128)S(1)} %copy-done.135, f32[24,512]{1,0:T(8,128)S(1)} %copy-done.218, ...), kind=kOutput, calls=%fused_computation.308 | convolution fusion | flops 4866441216 | bytes 15089760 | tf_op jit(solution)/shard_map/jvp(bhts,bshp->bthp)/dot_general | solution.py:79
  899.0 40.2 %fusion.45 = (f32[24,512]{1,0:T(8,128)}, f32[24,512]{1,0:T(8,128)}, f32[24,512]{1,0:T(8,128)S(1)}, f32[512,512]{1,0:T(8,128)}) fusion(f32[24,512]{1,0:T(8,128)S(1)} %copy-done.208, f32[512,512]{1,0:T(8,128)} %get-tuple-element.444, f32[24,512]{1,0:T(8,128)} %bitcast_add_fusion.31, f32[512,512]{1,0:T(8,128)S(1)} %copy-done.131, ...), kind=kOutput, calls=%fused_computation.51 | convolution fusion | flops 4925911040 | bytes 9945088 | tf_op jit(solution)/shard_map/transpose(jvp(bhts,bshp->bthp))/dot_general | solution.py:79
  939.3 24.4 %bitcast_add_fusion.2 = f32[1,512,24,64]{1,3,2,0:T(8,128)} fusion(f32[1,512,24,64]{1,3,2,0:T(8,128)S(1)} %bitcast.1290, f32[24,64,512]{2,1,0:T(8,128)S(1)} %bitcast.1289, f32[24,512]{1,0:T(8,128)S(1)} %copy-done.208, f32[512,512]{1,0:T(8,128)S(1)} %copy-done.138, f32[24,512]{1,0:T(8,128)S(1)} %copy-done.221, f32[512,512]{1,0:T(8,128)S(1)} %copy-done.131, ...), kind=kOutput, calls=%fused_computation.309 | convolution fusion | flops 4864868352 | bytes 11894880 | tf_op jit(solution)/shard_map/transpose(jvp(bhts,bshp->bthp))/dot_general | solution.py:79
  1042.0 7.0 fusion.312
  1057.8 16.9 collective-permute-done.16
  1100.1 40.2 %fusion.47 = (f32[24,512]{1,0:T(8,128)}, f32[24,512]{1,0:T(8,128)}, f32[24,512]{1,0:T(8,128)}, f32[512,512]{1,0:T(8,128)}) fusion(f32[24,512]{1,0:T(8,128)S(1)} %copy-done.206, f32[512,512]{1,0:T(8,128)} %get-tuple-element.357, f32[24,512]{1,0:T(8,128)} %bitcast_add_fusion.30, f32[512,512]{1,0:T(8,128)S(1)} %copy-done.129, ...), kind=kOutput, calls=%fused_computation.53 | convolution fusion | flops 4925911040 | bytes 9945088 | tf_op jit(solution)/shard_map/transpose(jvp(bhts,bshp->bthp))/dot_general | solution.py:79
  1141.5 24.4 %bitcast_add_fusion = f32[1,512,24,64]{1,3,2,0:T(8,128)} fusion(f32[1,512,24,64]{1,3,2,0:T(8,128)S(1)} %bitcast.1295, f32[24,64,512]{2,1,0:T(8,128)S(1)} %bitcast.1294, f32[24,512]{1,0:T(8,128)S(1)} %copy-done.207, f32[512,512]{1,0:T(8,128)S(1)} %copy-done.136, f32[24,512]{1,0:T(8,128)S(1)} %copy-done.219, f32[512,512]{1,0:T(8,128)S(1)} %copy-done.129, ...), kind=kOutput, calls=%fused_computation.306 | convolution fusion | flops 4864868352 | bytes 11894880 | tf_op jit(solution)/shard_map/transpose(jvp(bhts,bshp->bthp))/dot_general | solution.py:79
  1182.9 7.0 fusion.414
  1249.3 8.1 fusion.311
  1261.4 24.0 %fusion.129 = f32[1,768,3352]{1,2,0:T(8,128)} fusion(bf16[512,24]{1,0:T(8,128)(2,1)S(1)} %bitcast.1356, bf16[512,1792]{1,0:T(8,128)(2,1)} %copy-done.104, bf16[512,1536]{1,0:T(8,128)(2,1)} %get-tuple-element.306, bf16[512,24]{1,0:T(8,128)(2,1)S(1)} %bitcast.1354, bf16[512,1792]{1,0:T(8,128)(2,1)} %copy-done.103, bf16[512,1536]{1,0:T(8,128)(2,1)} %get-tuple-element.307, ...), kind=kOutput, calls=%fused_computation.135 | convolution fusion | flops 8008114176 | bytes 22953984 | tf_op jit(solution)/shard_map/rd,rk->dk/dot_general | solution.py:327
  1285.4 24.4 %copy.877 = f32[1,768,3352]{2,0,1:T(1,128)} copy(f32[1,768,3352]{1,2,0:T(8,128)} %fusion.129) | data formatting | bytes 20594688 | tf_op jit(solution)/shard_map/broadcast_in_dim | solution.py:345
  1311.8 8.1 fusion.150
  1329.9 29.2 %fusion.21 = f32[24,64,512]{2,1,0:T(8,128)S(1)} fusion(f32[512,24,64]{0,2,1:T(8,128)S(1)} %bitcast.1276, f32[24,512]{1,0:T(8,128)} %copy.778, f32[512,512]{1,0:T(8,128)} %get-tuple-element.416, f32[24,512]{1,0:T(8,128)S(1)} %bitcast_add_fusion.33, f32[512,512]{1,0:T(8,128)S(1)} %fusion.535, pred[512,512]{1,0:T(8,128)(4,1)} %get-tuple-element.415), kind=kOutput, calls=%fused_computation.27 | convolution fusion | flops 4863295488 | bytes 8749056 | tf_op jit(solution)/shard_map/bhts,bshp->bthp/dot_general | solution.py:79
  1381.0 30.2 %all-reduce.43 = (f32[1,24]{1,0:T(1,128)}, f32[1,24]{1,0:T(1,128)}, f32[1,24]{1,0:T(1,128)}) all-reduce(f32[1,24]{1,0:T(1,128)S(1)} %add_bitcast_fusion.2, f32[1,24]{1,0:T(1,128)S(1)} %bitcast_multiply_fusion.34, f32[1,24]{1,0:T(1,128)S(1)} %add_bitcast_fusion.1), channel_id=1, replica_groups=mesh['section'=2,'seq'=2,'dp'=8] {'seq','dp'}, use_global_device_ids=true, to_apply=%region_88.90 | all-reduce | flops 72 | bytes 576 | tf_op jit(solution)/shard_map/psum | solution.py:351
  1420.7 202.8 %all-reduce.47.cloned.1.call-done = f32[1,768,3352]{2,0,1:T(1,128)} async-done(((f32[1,768,3352]{2,0,1:T(1,128)}), f32[1,768,3352]{2,0,1:T(1,128)}) %all-reduce.47.cloned.1.call-update) | async-done | bytes 10297360
  1625.6 78.6 %reduce-scatter.14.cloned.1.call-done = f32[1,96,768]{2,1,0:T(8,128)} async-done(((f32[1,1536,768]{2,1,0:T(8,128)}), f32[1,96,768]{2,1,0:T(8,128)}) %reduce-scatter.14.cloned.1.call-update) | async-done | bytes 294928 | tf_op jit(solution)/shard_map/reduce_scatter | solution.py:349
  (1234 shorter events, 700.9 us)
Async XLA Ops:
  7.2 176.5 %all-gather.3.cloned.1.call-start = ((), (), s32[]{:S(2)}) async-start(), calls=%async_computation.5 | async-start | bytes 5640192 | tf_op jit(solution)/shard_map/all_gather | solution.py:253
  7.9 259.8 %all-gather.5.cloned.1.call-start = ((), (), s32[]{:S(2)}) async-start(), calls=%async_computation.6 | async-start | bytes 2506752 | tf_op jit(solution)/shard_map/all_gather | solution.py:257
  9.3 162.0 %collective-permute-start.9 = (f32[1,3]{1,0:T(1,128)S(1)}, f32[1,3]{1,0:T(1,128)S(1)}, u32[]{:S(2)}, u32[]{:S(2)}) collective-permute-start(f32[1,3]{1,0:T(1,128)S(1)} %slice.613), channel_id=1, source_target_pairs={{0,8},{1,9},{2,10},{3,11},{4,12},{5,13},{6,14},{7,15},{16,24},{17,... | collective-permute-start | bytes 44 | tf_op jit(solution)/shard_map/ppermute | solution.py:20
  11.8 157.7 %collective-permute-start.1 = (f32[1,3]{1,0:T(1,128)S(1)}, f32[1,3]{1,0:T(1,128)S(1)}, u32[]{:S(2)}, u32[]{:S(2)}) collective-permute-start(f32[1,3]{1,0:T(1,128)S(1)} %slice.571), channel_id=1, source_target_pairs={{0,8},{1,9},{2,10},{3,11},{4,12},{5,13},{6,14},{7,15},{16,24},{17,... | collective-permute-start | bytes 44 | tf_op jit(solution)/shard_map/ppermute | solution.py:20
  13.2 158.2 %collective-permute-start.5 = (f32[1,3]{1,0:T(1,128)S(1)}, f32[1,3]{1,0:T(1,128)S(1)}, u32[]{:S(2)}, u32[]{:S(2)}) collective-permute-start(f32[1,3]{1,0:T(1,128)S(1)} %slice.594), channel_id=1, source_target_pairs={{0,8},{1,9},{2,10},{3,11},{4,12},{5,13},{6,14},{7,15},{16,24},{17,... | collective-permute-start | bytes 44 | tf_op jit(solution)/shard_map/ppermute | solution.py:20
  14.5 1365.2 %reduce-scatter.22.cloned.1.call-start = ((), (), s32[]{:S(2)}) async-start(), calls=%async_computation.11 | async-start | bytes 835584
  84.8 498.3 %copy-start.145 = (f32[1536]{0:T(1024)}, f32[1536]{0:T(1024)S(1)}, u32[]{:S(2)}) copy-start(f32[1536]{0:T(1024)S(1)} %convert_element_type.570) | copy-start | bytes 18436
  86.3 425.5 %copy-start.170 = (f32[1792]{0:T(1024)}, f32[1792]{0:T(1024)S(1)}, u32[]{:S(2)}) copy-start(f32[1792]{0:T(1024)S(1)} %convert_element_type.568) | copy-start | bytes 21508
  166.4 345.3 %copy-start.158 = (f32[1792]{0:T(1024)}, f32[1792]{0:T(1024)S(1)}, u32[]{:S(2)}) copy-start(f32[1792]{0:T(1024)S(1)} %get-tuple-element.231) | copy-start | bytes 21508
  166.5 345.3 %copy-start.161 = (f32[1792]{0:T(1024)}, f32[1792]{0:T(1024)S(1)}, u32[]{:S(2)}) copy-start(f32[1792]{0:T(1024)S(1)} %get-tuple-element.232) | copy-start | bytes 21508
  166.5 345.3 %copy-start.164 = (f32[1792]{0:T(1024)}, f32[1792]{0:T(1024)S(1)}, u32[]{:S(2)}) copy-start(f32[1792]{0:T(1024)S(1)} %get-tuple-element.233) | copy-start | bytes 21508
  194.2 9.7 collective-permute-start
  223.3 31.6 %collective-permute-start.2 = (f32[1,24,64,128]{3,2,1,0:T(8,128)S(1)}, f32[1,24,64,128]{3,2,1,0:T(8,128)S(1)}, u32[]{:S(2)}, u32[]{:S(2)}) collective-permute-start(f32[1,24,64,128]{3,2,1,0:T(8,128)S(1)} %fusion.362), channel_id=1, source_target_pairs={{0,8},{1,9},{2,10},{3,11},{4,12},{5,13},{6,14},{7,15},{16,24},{17,... | collective-permute-start | bytes 2359304 | tf_op jit(solution)/shard_map/while/body/eval_jaxpr/ppermute | solution.py:20
  272.8 19.1 %collective-permute-start.3 = (bf16[1,512,768]{2,1,0:T(8,128)(2,1)S(1)}, bf16[1,512,768]{2,1,0:T(8,128)(2,1)S(1)}, u32[]{:S(2)}, u32[]{:S(2)}) collective-permute-start(bf16[1,512,768]{2,1,0:T(8,128)(2,1)S(1)} %fusion.354), channel_id=1, source_target_pairs={{0,16},{1,17},{2,18},{3,19},{4,20},{5,21},{6,22},{7,23},{8,24},{9,... | collective-permute-start | bytes 2359304 | tf_op jit(solution)/shard_map/ppermute | solution.py:20
  302.4 8.9 collective-permute-start.4
  331.9 29.4 %collective-permute-start.6 = (f32[1,24,64,128]{3,2,1,0:T(8,128)S(1)}, f32[1,24,64,128]{3,2,1,0:T(8,128)S(1)}, u32[]{:S(2)}, u32[]{:S(2)}) collective-permute-start(f32[1,24,64,128]{3,2,1,0:T(8,128)S(1)} %fusion.368), channel_id=1, source_target_pairs={{0,8},{1,9},{2,10},{3,11},{4,12},{5,13},{6,14},{7,15},{16,24},{17,... | collective-permute-start | bytes 2359304 | tf_op jit(solution)/shard_map/while/body/eval_jaxpr/ppermute | solution.py:20
  379.4 19.7 %collective-permute-start.7 = (bf16[1,512,768]{2,1,0:T(8,128)(2,1)S(1)}, bf16[1,512,768]{2,1,0:T(8,128)(2,1)S(1)}, u32[]{:S(2)}, u32[]{:S(2)}) collective-permute-start(bf16[1,512,768]{2,1,0:T(8,128)(2,1)S(1)} %fusion.318), channel_id=1, source_target_pairs={{0,16},{1,17},{2,18},{3,19},{4,20},{5,21},{6,22},{7,23},{8,24},{9,... | collective-permute-start | bytes 2359304 | tf_op jit(solution)/shard_map/ppermute | solution.py:20
  428.8 53.3 %collective-permute-start.8 = (f32[1,3,1792]{2,0,1:T(1,128)}, f32[1,3,1792]{2,0,1:T(1,128)}, u32[]{:S(2)}, u32[]{:S(2)}) collective-permute-start(f32[1,3,1792]{2,0,1:T(1,128)} %copy.772), channel_id=1, source_target_pairs={{0,8},{1,9},{2,10},{3,11},{4,12},{5,13},{6,14},{7,15},{16,24},{17,... | collective-permute-start | bytes 64520 | tf_op jit(solution)/shard_map/ppermute | solution.py:20
  504.3 32.1 %collective-permute-start.10 = (f32[1,24,64,128]{3,2,1,0:T(8,128)}, f32[1,24,64,128]{3,2,1,0:T(8,128)}, u32[]{:S(2)}, u32[]{:S(2)}) collective-permute-start(f32[1,24,64,128]{3,2,1,0:T(8,128)} %fusion.374), channel_id=1, source_target_pairs={{0,8},{1,9},{2,10},{3,11},{4,12},{5,13},{6,14},{7,15},{16,24},{17,... | collective-permute-start | bytes 2359304 | tf_op jit(solution)/shard_map/while/body/eval_jaxpr/ppermute | solution.py:20
  604.3 131.5 %collective-permute-start.11 = (f32[1,24,64,128]{3,2,1,0:T(8,128)}, f32[1,24,64,128]{3,2,1,0:T(8,128)}, u32[]{:S(2)}, u32[]{:S(2)}) collective-permute-start(f32[1,24,64,128]{3,2,1,0:T(8,128)} %fusion.379), channel_id=1, source_target_pairs={{8,0},{9,1},{10,2},{11,3},{12,4},{13,5},{14,6},{15,7},{24,16},{25,... | collective-permute-start | bytes 2359304 | tf_op jit(solution)/shard_map/while/body/eval_jaxpr/ppermute | solution.py:20
  796.9 20.8 %collective-permute-start.12 = (f32[1,3,1792]{2,0,1:T(1,128)S(1)}, f32[1,3,1792]{2,0,1:T(1,128)S(1)}, u32[]{:S(2)}, u32[]{:S(2)}) collective-permute-start(f32[1,3,1792]{2,0,1:T(1,128)S(1)} %copy.804), channel_id=1, source_target_pairs={{8,0},{9,1},{10,2},{11,3},{12,4},{13,5},{14,6},{15,7},{24,16},{25,... | collective-permute-start | bytes 64520 | tf_op jit(solution)/shard_map/ppermute | solution.py:20
  829.2 38.8 %collective-permute-start.13 = (bf16[1,512,768]{2,1,0:T(8,128)(2,1)}, bf16[1,512,768]{2,1,0:T(8,128)(2,1)}, u32[]{:S(2)}, u32[]{:S(2)}) collective-permute-start(bf16[1,512,768]{2,1,0:T(8,128)(2,1)} %get-tuple-element.286), channel_id=1, source_target_pairs={{16,0},{17,1},{18,2},{19,3},{20,4},{21,5},{22,6},{23,7},{24,8},{25... | collective-permute-start | bytes 2359304 | tf_op jit(solution)/shard_map/ppermute | solution.py:20
  897.7 87.2 %collective-permute-start.14 = (f32[1,24,64,128]{3,2,1,0:T(8,128)}, f32[1,24,64,128]{3,2,1,0:T(8,128)}, u32[]{:S(2)}, u32[]{:S(2)}) collective-permute-start(f32[1,24,64,128]{3,2,1,0:T(8,128)} %fusion.378), channel_id=1, source_target_pairs={{8,0},{9,1},{10,2},{11,3},{12,4},{13,5},{14,6},{15,7},{24,16},{25,... | collective-permute-start | bytes 2359304 | tf_op jit(solution)/shard_map/while/body/eval_jaxpr/ppermute | solution.py:20
  1034.5 4.8 collective-permute-start.15
  1052.6 22.1 %collective-permute-start.16 = (bf16[1,512,768]{2,1,0:T(8,128)(2,1)S(1)}, bf16[1,512,768]{2,1,0:T(8,128)(2,1)S(1)}, u32[]{:S(2)}, u32[]{:S(2)}) collective-permute-start(bf16[1,512,768]{2,1,0:T(8,128)(2,1)S(1)} %convert_element_type.548), channel_id=1, source_target_pairs={{16,0},{17,1},{18,2},{19,3},{20,4},{21,5},{22,6},{23,7},{24,8},{25... | collective-permute-start | bytes 2359304 | tf_op jit(solution)/shard_map/ppermute | solution.py:20
  1098.5 91.4 %collective-permute-start.17 = (f32[1,24,64,128]{3,2,1,0:T(8,128)}, f32[1,24,64,128]{3,2,1,0:T(8,128)}, u32[]{:S(2)}, u32[]{:S(2)}) collective-permute-start(f32[1,24,64,128]{3,2,1,0:T(8,128)} %fusion.377), channel_id=1, source_target_pairs={{8,0},{9,1},{10,2},{11,3},{12,4},{13,5},{14,6},{15,7},{24,16},{25,... | collective-permute-start | bytes 2359304 | tf_op jit(solution)/shard_map/while/body/eval_jaxpr/ppermute | solution.py:20
  1176.4 234.8 %reduce-scatter.20.cloned.1.call-start = ((), (), s32[]{:S(2)}) async-start(), calls=%async_computation.10 | async-start | bytes 974848
  1239.3 7.4 collective-permute-start.18
  1244.7 173.2 %reduce-scatter.16.cloned.1.call-start = ((), (), s32[]{:S(2)}) async-start(), calls=%async_computation.8 | async-start | bytes 417792
  1258.4 160.8 %reduce-scatter.18.cloned.1.call-start = ((), (), s32[]{:S(2)}) async-start(), calls=%async_computation.9 | async-start | bytes 974848
  1261.3 362.2 %all-reduce.47.cloned.1.call-start = ((), (), s32[]{:S(2)}) async-start(), calls=%async_computation.12 | async-start | bytes 21233664
  1309.9 394.2 %reduce-scatter.14.cloned.1.call-start = ((), (), s32[]{:S(2)}) async-start(), calls=%async_computation.7 | async-start | bytes 5013504 | tf_op jit(solution)/shard_map/reduce_scatter | solution.py:349
  (367 other events, 4367.4 us)
Sparse Core Ops, SparseCore 0:
  10.2 59.9 all-gather.2
  72.5 45.4 all-gather.4
  1176.6 54.3 reduce-scatter.21
  1244.8 54.8 reduce-scatter.19
  1303.6 54.5 reduce-scatter.15
  1362.0 56.1 reduce-scatter.17
  1422.0 201.4 all-reduce.46
  1628.4 75.6 reduce-scatter.13
where the time goes:
time: 1730 us; the launch traced here: 1710 us
  matrix products  615 us (36%)
  waiting for transfers between devices  313 us (18%)
  other arithmetic  304 us (18%)
  local copies, waits for them, and re-layouts  281 us (16%)
  blocking collectives  133 us (8%)
  starting transfers between devices  34.2 us (2%)
  between operations  30.1 us (2%)
    dot_general x12, matrix products, out_part(): result = jnp.einsum('bhts,bshp->bthp', mixing, heads_x, precision=highest)  373 us
    unnamed x13, waiting for transfers between devices  204 us
    reduce_scatter x1, waiting for transfers between devices, shards(): lax.psum_scatter(grad_out_weight[None], ('seq', 'dp'), scatter_dimension=...  78.6 us
    unnamed x1, blocking collectives  62.7 us
    dot_general x12, matrix products, out_part(): jnp.einsum('bhpn,btn->bthp', incoming, c_in, precision=highest)  62.4 us
    another operation x36, other arithmetic  51.7 us
    dot_general x9, matrix products, state_part(): jnp.einsum('bsh,bshp,bsn->bhpn', tail_weight, heads_x, b_in, precision=hi...  47.6 us
    all_gather x1, blocking collectives, shards(): lax.all_gather(packed[2], ('seq', 'dp'), axis=2, tiled=True)  40 us
  transfers between devices with their start and end apart: 27, of which 6 were waited for; matrix products, arithmetic and copies ran while one was open for 49% of the time, Pallas kernels for 0%

commit v1 on v0

v1 whole, which is shorter than its diff:
```python
from functools import partial

import jax
import jax.numpy as jnp
from jax import lax
from jax.experimental import pallas as pl
from jax.experimental.pallas import tpu as pltpu
from jax.sharding import PartitionSpec as P

DI = 1536
N = 128
XC = 1792
EPS = 1e-05
MASKED = -1e30
VMEM_LIMIT = 40 * 1024 * 1024
LANES = 128

f32 = jnp.float32
bf16 = jnp.bfloat16
highest = lax.Precision.HIGHEST


def dot(a, b, contract=((1,), (0,)), precision=None):
    return lax.dot_general(
        a, b, (contract, ((), ())), precision=precision, preferred_element_type=f32
    )


ROWS = ((1,), (1,))
COLS = ((0,), (0,))


def split3(v):
    hi = v.astype(bf16)
    rest = v - hi.astype(f32)
    mid = rest.astype(bf16)
    return hi, mid, (rest - mid.astype(f32)).astype(bf16)


def widen(v, expand):
    return dot(jnp.concatenate(split3(v), 1), expand)


def narrow(v, reduce):
    return dot(v.astype(bf16), reduce)


def narrow_exact(v, reduce):
    hi, mid, lo = split3(v)
    return dot(hi, reduce) + dot(mid, reduce) + dot(lo, reduce)


def sigmoid(v):
    return 1.0 / (1.0 + jnp.exp(-v))


def softplus(v):
    return jnp.maximum(v, 0.0) + jnp.log1p(jnp.exp(-jnp.abs(v)))


def conv_forward(pad, match, convp, rows):
    out = convp[4:5, :] + convp[3:4, :] * pad[8 : 8 + rows, :]
    for k in range(3):
        out = out + convp[k : k + 1, :] * pad[5 + k : 5 + k + rows, :] * match[:, k : k + 1]
    return out


def half_masks(rows):
    lane = lax.broadcasted_iota(jnp.int32, (rows, LANES), 1)
    low = jnp.where(lane < LANES // 2, 1.0, 0.0)
    return low.astype(bf16), (1.0 - low).astype(bf16)


def prep_kernel(
    proj, rim, match, convp, headp, expand, xt_o, xs_o, bc_o, cum_o, cumt_o, sin_o, end_o, pref_o,
    thru_o, pad, state, pref,
):
    c = pl.program_id(0)
    rows = proj.shape[0]
    heads = headp.shape[1]

    @pl.when(c == 0)
    def _():
        pad[0:8, :] = rim[...]
        state[...] = jnp.zeros_like(state)
        pref[...] = jnp.ones_like(pref)

    @pl.when(c > 0)
    def _():
        pad[0:8, :] = pad[rows : rows + 8, :]

    pad[8 : 8 + rows, :] = proj[:, DI : DI + XC]
    m = match[...]
    conv = conv_forward(pad, m, convp, rows)
    act = conv * sigmoid(conv)
    dt = softplus(proj[:, DI + XC :] + headp[0:1, :])
    log_decay = dt * headp[1:2, :]
    row = lax.broadcasted_iota(jnp.int32, (rows, rows), 0)
    col = lax.broadcasted_iota(jnp.int32, (rows, rows), 1)
    lower = jnp.where(row >= col, 1.0, 0.0)
    cum = dot(lower, log_decay, precision=highest)
    cum_o[...] = cum
    cumt_o[0] = dot(
        log_decay, jnp.where(row <= col, 1.0, 0.0), COLS, precision=highest
    )
    last = cum[rows - 1 : rows, :]
    wide = widen(
        jnp.concatenate(
            [dt, jnp.exp(last - cum) * m[:, 5:6],
             jnp.broadcast_to(jnp.exp(last) * m[rows - 1 : rows, 4:5], (8, heads))], 0
        ),
        expand[...],
    )
    x = act[:, :DI]
    xt = x * wide[:rows]
    b = act[:, DI : DI + N].astype(bf16)
    xt_o[...] = xt.astype(bf16)
    xs_o[...] = x.astype(bf16)
    bc_o[...] = act[:, DI:].astype(bf16)
    sin_o[0] = state[...].astype(bf16)
    pref_o[0] = pref[...]
    through = wide[2 * rows :]
    state[...] = through[0:1] * state[...] + dot(
        b, (xt * wide[rows : 2 * rows]).astype(bf16), COLS
    )
    pref[...] = pref[...] * through
    end_o[...] = state[...]
    thru_o[...] = pref[...]


def decay_mask(seg_col, seg_row, transposed):
    rows = seg_col.shape[0]
    row = lax.broadcasted_iota(jnp.int32, (rows, rows), 0)
    col = lax.broadcasted_iota(jnp.int32, (rows, rows), 1)
    order = (col >= row) if transposed else (row >= col)
    return (seg_col == seg_row) & order


def intra_kernel(xt, bc, cum, cumt, match, segt, yi_o):
    rows = xt.shape[0]
    mask = decay_mask(match[:, 3:4], segt[0], False)
    scores = dot(bc[:, N:], bc[:, :N], ROWS)
    low, high = half_masks(rows)
    for p in range(xt.shape[1] // LANES):
        mixes = []
        for h in (2 * p, 2 * p + 1):
            gap = cum[:, h : h + 1] - cumt[0, h : h + 1, :]
            mixes.append((jnp.exp(jnp.where(mask, gap, MASKED)) * scores).astype(bf16))
        xp = xt[:, LANES * p : LANES * (p + 1)]
        blocks = jnp.concatenate([xp * low, xp * high], 0)
        yi_o[:, LANES * p : LANES * (p + 1)] = dot(jnp.concatenate(mixes, 1), blocks)


def finish_kernel(
    yi, xs, bc, cum, match, sin_l, pref, dev, z_ref, gains, expand, y_o, no_o, sin_o
):
    sin = (sin_l[0].astype(f32) + pref[0, 0:1, :] * dev[...]).astype(bf16)
    sin_o[0] = sin
    carry = widen(jnp.exp(cum[...]) * match[:, 4:5], expand[...])
    y = yi[...] + carry * dot(bc[:, N:], sin) + gains[1:2, :] * xs[...].astype(f32)
    y_o[...] = y
    z = z_ref[...]
    g = y * z * sigmoid(z)
    r = lax.rsqrt(jnp.mean(g * g, -1, keepdims=True) + EPS)
    no_o[...] = (g * r * gains[0:1, :]).astype(bf16)


def gate_back_kernel(
    gno, y_ref, z_ref, gains, cum, match, bc, pref, expand, dy_o, dz_o, edy_o, og_o, ds_o
):
    @pl.when(pl.program_id(0) == 0)
    def _():
        og_o[...] = jnp.zeros_like(og_o)
        ds_o[...] = jnp.zeros_like(ds_o)

    z = z_ref[...]
    y = y_ref[...]
    sz = sigmoid(z)
    silu = z * sz
    g = y * silu
    r = lax.rsqrt(jnp.mean(g * g, -1, keepdims=True) + EPS)
    gr = g * r
    gv = gno[...]
    og_o[...] += jnp.broadcast_to(jnp.sum(gv * gr, 0, keepdims=True), og_o.shape)
    gn = gv * gains[0:1, :]
    dg = r * (gn - gr * jnp.mean(gn * gr, -1, keepdims=True))
    dy = dg * silu
    dy_o[...] = dy.astype(bf16)
    dz_o[...] = (dg * y * sz * (1.0 + z * (1.0 - sz))).astype(bf16)
    edy = (widen(jnp.exp(cum[...]) * match[:, 4:5], expand[...]) * dy).astype(bf16)
    edy_o[...] = edy
    ds_o[...] += pref[0, 0:1, :] * dot(bc[:, N:], edy, COLS)


def intra_back_kernel(
    dy, xt, bc, cum, cumt, match, segt, reduce, dxi_o, dbc_o, dcum_o, rs
):
    rows = xt.shape[0]
    mask = decay_mask(match[:, 3:4], segt[0], True)
    b = bc[:, :N]
    c = bc[:, N:]
    scores = dot(b, c, ROWS)
    low, high = half_masks(rows)
    rs[...] = jnp.zeros_like(rs)
    dscores = jnp.zeros((rows, rows), f32)
    for p in range(xt.shape[1] // LANES):
        xp = xt[:, LANES * p : LANES * (p + 1)]
        dyp = dy[:, LANES * p : LANES * (p + 1)]
        dmix = dot(jnp.concatenate([xp * low, xp * high], 0), dyp, ROWS)
        mixes = []
        for j in range(2):
            h = 2 * p + j
            gap = cumt[0, h : h + 1, :] - cum[:, h : h + 1]
            decay = jnp.exp(jnp.where(mask, gap, MASKED))
            dm = dmix[rows * j : rows * (j + 1)]
            dscores = dscores + dm * decay
            mix = (decay * scores).astype(bf16)
            mixes.append(mix)
            rs[h : h + 1, :] = jnp.sum(dm * mix.astype(f32), 0, keepdims=True)
        blocks = jnp.concatenate([dyp * low, dyp * high], 0)
        dxi_o[:, LANES * p : LANES * (p + 1)] = dot(jnp.concatenate(mixes, 1), blocks)
    ds = dscores.astype(bf16)
    dbc_o[:, :N] = dot(ds, c)
    dbc_o[:, N:] = dot(ds, b, COLS)
    heads = cum.shape[1]
    cols = narrow_exact(xt[...].astype(f32) * dxi_o[...], reduce[...])
    dcum_o[...] = jnp.transpose(rs[...])[:, :heads] - cols


def sweep_kernel(
    dxi, dbc, dcum, dy, edy, dz, xt, bc, cum, match, sin_ref, proj, before, rim, convp, headp,
    gains, expand, reduce, dsn, gp_o, convg_o, headg_o, rim_o, ds, pad, buf, carry, acc,
):
    i = pl.program_id(0)
    steps = pl.num_programs(0)
    rows = xt.shape[0]
    heads = cum.shape[1]

    @pl.when(i == 0)
    def _():
        ds[...] = dsn[...]
        carry[...] = jnp.zeros_like(carry)
        convg_o[...] = jnp.zeros_like(convg_o)
        headg_o[...] = jnp.zeros_like(headg_o)

    @pl.when(i == steps - 1)
    def _():
        pad[0:8, :] = rim[...]

    @pl.when(i < steps - 1)
    def _():
        pad[0:8, :] = before[:, DI : DI + XC]

    pad[8 : 8 + rows, :] = proj[:, DI : DI + XC]
    m = match[...]
    conv = conv_forward(pad, m, convp, rows)
    sc = sigmoid(conv)
    act = conv * sc
    x = act[:, :DI]
    raw = proj[:, DI + XC :] + headp[0:1, :]
    dt = softplus(raw)
    rate = headp[1:2, :]
    cumv = cum[...]
    last = cumv[rows - 1 : rows, :]
    thru = jnp.exp(last) * m[rows - 1 : rows, 4:5]
    wide = widen(
        jnp.concatenate(
            [dt, jnp.exp(last - cumv) * m[:, 5:6], jnp.broadcast_to(thru, (8, heads))], 0
        ),
        expand[...],
    )
    dt_e = wide[:rows]
    tail_e = wide[rows : 2 * rows]
    thru_e = wide[2 * rows : 2 * rows + 1]
    b = bc[:, :N]
    c = bc[:, N:]
    state_grad = ds[...]
    low_grad = state_grad.astype(bf16)
    sin = sin_ref[0]
    xtv = xt[...].astype(f32)
    dyv = dy[...].astype(f32)
    edyb = edy[...]
    dx_in = tail_e * dot(b, low_grad)
    dxt = dxi[...] + dx_in
    stacked = jnp.concatenate(
        [
            (xtv * dx_in).astype(bf16),
            (edyb.astype(f32) * dot(c, sin)).astype(bf16),
            (x * dxt).astype(bf16),
            (x * dyv).astype(bf16),
        ],
        0,
    )
    sums = dot(stacked, reduce[...])
    db = dbc[:, :N] + dot((tail_e * xtv).astype(bf16), low_grad, ROWS)
    dc = dbc[:, N:] + dot(edyb, sin, ROWS)
    held = jnp.sum(state_grad * sin.astype(f32), 0, keepdims=True)
    dthru = narrow_exact(jnp.broadcast_to(held, (8, held.shape[1])), reduce[...])[0:1] * thru
    ds[...] = thru_e * state_grad + dot(c, edyb, COLS)
    row = lax.broadcasted_iota(jnp.int32, (rows, rows), 0)
    col = lax.broadcasted_iota(jnp.int32, (rows, rows), 1)
    dlog = (
        dot(jnp.where(row <= col, 1.0, 0.0), dcum[...] + sums[rows : 2 * rows], precision=highest)
        + dot(jnp.where(row > col, 1.0, 0.0), sums[:rows], precision=highest)
        + dthru
    )
    ddt = sums[2 * rows : 3 * rows] + dlog * rate
    draw = ddt * sigmoid(raw)
    headg_o[0:1, :] += jnp.sum(draw, 0, keepdims=True)
    headg_o[1:2, :] += jnp.sum(dlog * dt, 0, keepdims=True) * rate
    headg_o[2:3, :] += jnp.sum(sums[3 * rows :], 0, keepdims=True)
    gp_o[:, :DI] = dz[...]
    gp_o[:, DI + XC :] = draw.astype(bf16)
    dact = jnp.concatenate([dt_e * dxt + gains[1:2, :] * dyv, db, dc], 1)
    dconv = dact * (sc * (1.0 + conv * (1.0 - sc)))
    convg_o[4:5, :] += jnp.sum(dconv, 0, keepdims=True)
    convg_o[3:4, :] += jnp.sum(dconv * pad[8 : 8 + rows, :], 0, keepdims=True)
    acc[...] = dconv * convp[3:4, :]
    rim_sum = jnp.zeros((8, XC), f32)
    for k in range(3):
        v = dconv * m[:, k : k + 1]
        convg_o[k : k + 1, :] += jnp.sum(v * pad[5 + k : 5 + k + rows, :], 0, keepdims=True)
        v = v * convp[k : k + 1, :]
        buf[0:8, :] = jnp.zeros((8, XC), f32)
        buf[8 : 8 + rows, :] = v
        buf[8 + rows : 16 + rows, :] = carry[8 * k : 8 * k + 8, :]
        shift = 3 - k
        acc[...] += buf[8 + shift : 8 + shift + rows, :]
        rim_sum = rim_sum + buf[shift : 8 + shift, :]
        carry[8 * k : 8 * k + 8, :] = v[0:8, :]
    gp_o[:, DI : DI + XC] = acc[...].astype(bf16)
    rim_o[...] = rim_sum


def shapes(*specs):
    return [jax.ShapeDtypeStruct(s, d) for s, d in specs]


def by_chunk(rows, cols, steps=None):
    if steps is None:
        return pl.BlockSpec((rows, cols), lambda i: (i, 0))
    return pl.BlockSpec((rows, cols), lambda i: (steps - 1 - i, 0))


def by_lead(a, b, steps=None):
    if steps is None:
        return pl.BlockSpec((1, a, b), lambda i: (i, 0, 0))
    return pl.BlockSpec((1, a, b), lambda i: (steps - 1 - i, 0, 0))


def fixed(*shape):
    return pl.BlockSpec(shape, lambda i: (0,) * len(shape))


def call(kernel, steps, ins, outs, out_shape, scratch=(), flops=0, moved=0):
    return pl.pallas_call(
        kernel,
        grid=(steps,),
        in_specs=ins,
        out_specs=outs,
        out_shape=out_shape,
        scratch_shapes=scratch,
        compiler_params=pltpu.CompilerParams(
            dimension_semantics=("arbitrary",), vmem_limit_bytes=VMEM_LIMIT
        ),
        cost_estimate=pl.CostEstimate(flops=flops, bytes_accessed=moved, transcendentals=0),
    )


def shifted(value, axis, steps):
    count = lax.axis_size(axis)
    initial, last = (max(0, -steps), min(count, count - steps))
    return lax.ppermute(value, axis, [(source, source + steps) for source in range(initial, last)])


def relay(through, local, steps):
    incoming = shifted(local, "seq", steps)
    for _ in range(lax.axis_size("seq") - 2):
        incoming = shifted(through[0:1] * incoming + local, "seq", steps)
    return incoming


def rms_scale(values, gain):
    return values * lax.rsqrt(jnp.mean(values * values, -1, keepdims=True) + EPS) * gain


def layer_forward(source, w, seg):
    match, segt, rows = seg["match"], seg["segt"], seg["rows"]
    T = source.shape[0]
    nc = T // rows
    H = w["headp"].shape[1]
    PWL = w["win"].shape[1]
    normed = rms_scale(source, w["norm_gain"]).astype(bf16)
    proj = dot(normed, w["win"])
    rim = shifted(proj[-8:, DI : DI + XC], "seq", 1)
    expand = seg["expand"]
    xt, xs, bc, cum, cumt, sin_l, end, pref, thru = call(
        prep_kernel,
        nc,
        [by_chunk(rows, PWL), fixed(8, XC), by_chunk(rows, 8), fixed(8, XC), fixed(8, H),
         fixed(*expand.shape)],
        [by_chunk(rows, DI), by_chunk(rows, DI), by_chunk(rows, 2 * N), by_chunk(rows, H),
         by_lead(H, rows), by_lead(N, DI), fixed(N, DI), by_lead(8, DI), fixed(8, DI)],
        shapes(((T, DI), bf16), ((T, DI), bf16), ((T, 2 * N), bf16), ((T, H), f32),
               ((nc, H, rows), f32), ((nc, N, DI), bf16), ((N, DI), f32), ((nc, 8, DI), f32),
               ((8, DI), f32)),
        [pltpu.VMEM((rows + 8, XC), f32), pltpu.VMEM((N, DI), f32), pltpu.VMEM((8, DI), f32)],
        flops=int(2e9), moved=int(1.5e7),
    )(proj, rim, match, w["convp"], w["headp"], expand)
    dev = relay(thru, end, 1)
    yi = call(
        intra_kernel,
        nc,
        [by_chunk(rows, DI), by_chunk(rows, 2 * N), by_chunk(rows, H), by_lead(H, rows),
         by_chunk(rows, 8), by_lead(1, rows)],
        by_chunk(rows, DI),
        jax.ShapeDtypeStruct((T, DI), f32),
        flops=int(8e9), moved=int(5e6),
    )(xt, bc, cum, cumt, match, segt)
    y, normed_out, sin = call(
        finish_kernel,
        nc,
        [by_chunk(rows, DI), by_chunk(rows, DI), by_chunk(rows, 2 * N), by_chunk(rows, H),
         by_chunk(rows, 8), by_lead(N, DI), by_lead(8, DI), fixed(N, DI), by_chunk(rows, DI),
         fixed(8, DI), fixed(*expand.shape)],
        [by_chunk(rows, DI), by_chunk(rows, DI), by_lead(N, DI)],
        shapes(((T, DI), f32), ((T, DI), bf16), ((nc, N, DI), bf16)),
        flops=int(2e9), moved=int(1.5e7),
    )(yi, xs, bc, cum, match, sin_l, pref, dev, proj, w["gains"], expand)
    out = source + dot(normed_out, w["wout"])
    kept = dict(
        source=source, normed=normed, proj=proj, rim=rim, xt=xt, bc=bc, cum=cum, cumt=cumt,
        pref=pref, thru=thru, y=y, normed_out=normed_out, sin=sin,
    )
    return out, kept


def layer_backward(grad_low, w, seg, kept):
    match, segt, rows = seg["match"], seg["segt"], seg["rows"]
    T = grad_low.shape[0]
    nc = T // rows
    H = w["headp"].shape[1]
    PWL = w["win"].shape[1]
    expand, reduce = seg["expand"], seg["reduce"]
    proj, bc, cum, xt = kept["proj"], kept["bc"], kept["cum"], kept["xt"]
    gno = dot(grad_low, w["wout"], ROWS)
    dy, dz, edy, og, ds_local = call(
        gate_back_kernel,
        nc,
        [by_chunk(rows, DI), by_chunk(rows, DI), by_chunk(rows, DI), fixed(8, DI),
         by_chunk(rows, H), by_chunk(rows, 8), by_chunk(rows, 2 * N), by_lead(8, DI),
         fixed(*expand.shape)],
        [by_chunk(rows, DI), by_chunk(rows, DI), by_chunk(rows, DI), fixed(8, DI), fixed(N, DI)],
        shapes(((T, DI), bf16), ((T, DI), bf16), ((T, DI), bf16), ((8, DI), f32), ((N, DI), f32)),
        flops=int(2e9), moved=int(1.5e7),
    )(gno, kept["y"], proj, w["gains"], cum, match, bc, kept["pref"], expand)
    dsn = relay(kept["thru"], ds_local, -1)
    dxi, dbc, dcum = call(
        intra_back_kernel,
        nc,
        [by_chunk(rows, DI), by_chunk(rows, DI), by_chunk(rows, 2 * N), by_chunk(rows, H),
         by_lead(H, rows), by_chunk(rows, 8), by_lead(1, rows), fixed(*reduce.shape)],
        [by_chunk(rows, DI), by_chunk(rows, 2 * N), by_chunk(rows, H)],
        shapes(((T, DI), f32), ((T, 2 * N), f32), ((T, H), f32)),
        [pltpu.VMEM((LANES, rows), f32)],
        flops=int(2e10), moved=int(1e7),
    )(dy, xt, bc, cum, kept["cumt"], match, segt, reduce)
    rc = functools_rev(rows, nc)
    gp, convg, headg, rim_grad = call(
        sweep_kernel,
        nc,
        [rc(DI), rc(2 * N), rc(H), rc(DI), rc(DI), rc(DI), rc(DI), rc(2 * N), rc(H), rc(8),
         by_lead(N, DI, nc), rc(PWL),
         pl.BlockSpec((8, PWL), lambda i: (jnp.maximum((nc - 1 - i) * (rows // 8) - 1, 0), 0)),
         fixed(8, XC), fixed(8, XC), fixed(8, H), fixed(8, DI), fixed(*expand.shape),
         fixed(*reduce.shape), fixed(N, DI)],
        [rc(PWL), fixed(8, XC), fixed(8, H), fixed(8, XC)],
        shapes(((T, PWL), bf16), ((8, XC), f32), ((8, H), f32), ((8, XC), f32)),
        [pltpu.VMEM((N, DI), f32), pltpu.VMEM((rows + 8, XC), f32),
         pltpu.VMEM((rows + 16, XC), f32), pltpu.VMEM((24, XC), f32),
         pltpu.VMEM((rows, XC), f32)],
        flops=int(4e9), moved=int(2e7),
    )(dxi, dbc, dcum, dy, edy, dz, xt, bc, cum, match, kept["sin"], proj, proj, kept["rim"],
      w["convp"], w["headp"], w["gains"], expand, reduce, dsn)
    returned = shifted(rim_grad, "seq", -1)
    tail = (gp[-16:, DI : DI + XC].astype(f32)
            + jnp.concatenate([jnp.zeros_like(returned), returned], 0)).astype(bf16)
    gp = lax.dynamic_update_slice(gp, tail, (T - 16, DI))
    grad_normed = dot(gp, w["win"], ROWS)
    _, norm_pull = jax.vjp(rms_scale, kept["source"], w["norm_gain"])
    grad_source, grad_norm_gain = norm_pull(grad_normed)
    grad_in = dot(kept["normed"], gp, COLS)
    grad_out = dot(kept["normed_out"], grad_low, COLS)
    return grad_source, (grad_in, grad_out, grad_norm_gain, convg, og[0], headg)


def functools_rev(rows, nc):
    return lambda cols: by_chunk(rows, cols, nc)


def seg_tables(segments, rows, heads):
    T = segments.shape[0]
    seg = segments.astype(f32)
    rim = shifted(seg[-3:], "seq", 1)
    padded = jnp.concatenate([rim, seg])
    cols = [(padded[k : k + T] == seg).astype(f32) for k in range(3)]
    chunked = seg.reshape(-1, rows)
    ends = chunked[:, -1]
    starts = jnp.concatenate([rim[-1:], ends[:-1]])
    cols.append(seg)
    cols.append((chunked == starts[:, None]).astype(f32).reshape(-1))
    cols.append((chunked == ends[:, None]).astype(f32).reshape(-1))
    match = jnp.stack(cols + [jnp.zeros_like(seg)] * 2, 1)
    head_of = jnp.arange(DI) // (DI // heads)
    one = (jnp.arange(heads)[:, None] == head_of[None, :]).astype(bf16)
    return dict(
        match=match, segt=chunked[:, None, :], rows=rows,
        expand=jnp.concatenate([one, one, one], 0), reduce=one.T,
    )


def shards(
    tokens, cotangent, segments, norm_gain, in_weight, conv_weight, conv_bias, dt_bias, decay_log,
    skip_gain, out_gain, out_weight,
):
    section = lax.axis_index("section")
    is_first = section == 0
    D = tokens.shape[-1]
    H = dt_bias.shape[-1]
    T = tokens.shape[2]
    rows = min(LANES, T)
    cut = conv_weight.shape[-1]
    everyone = ("section", "seq", "dp")
    mine = partial(lax.dynamic_index_in_dim, index=section, axis=0, keepdims=False)
    source = mine(tokens)[0]
    grad_low = mine(cotangent)[0]
    seg = seg_tables(mine(segments)[0], rows, H)

    small = jnp.concatenate(
        [norm_gain[0], conv_weight[0].reshape(-1), conv_bias[0], out_gain[0]]
    )[None]
    small = lax.all_gather(small, everyone, axis=0, tiled=True)
    small = small.reshape(2, -1, small.shape[-1]).astype(f32)
    heads_own = jnp.concatenate([dt_bias, -jnp.exp(decay_log), skip_gain], 0)
    heads_other = lax.ppermute(heads_own, "section", [(0, 1), (1, 0)])
    win = lax.all_gather(in_weight, everyone, axis=1, tiled=True).reshape(2, D, -1)
    wout = lax.all_gather(out_weight, everyone, axis=1, tiled=True).reshape(2, DI, D)
    weights = []
    nd, no = norm_gain.shape[-1], out_gain.shape[-1]
    for s in range(2):
        vec = small[s]
        heads = jnp.where(section == s, heads_own, heads_other)
        taps = vec[:, nd : nd + 4 * cut].reshape(-1, 4, cut)
        taps = jnp.swapaxes(taps, 0, 1).reshape(4, -1)
        bias = vec[:, nd + 4 * cut : nd + 5 * cut].reshape(1, -1)
        gain = vec[:, nd + 5 * cut :].reshape(1, -1)
        skip = jnp.repeat(heads[2], DI // H)[None]
        weights.append(dict(
            norm_gain=vec[:, :nd].reshape(-1),
            convp=jnp.concatenate([taps, bias, jnp.zeros((3, XC), f32)], 0),
            headp=jnp.concatenate([heads, jnp.zeros((5, H), f32)], 0),
            gains=jnp.concatenate([gain, skip, jnp.zeros((6, DI), f32)], 0),
            win=win[s], wout=wout[s],
        ))

    swap = [(0, 1), (1, 0)]
    out0, kept0 = layer_forward(source.astype(f32), weights[0], seg)
    passed = out0.astype(bf16)
    out1, kept1 = layer_forward(passed.astype(f32), weights[1], seg)
    final = out1.astype(bf16)
    got = lax.ppermute(jnp.where(is_first, final, passed), "section", swap)
    own = jnp.where(is_first, passed, final)
    section_outputs = jnp.where(is_first, jnp.stack([own, got]), jnp.stack([got, own]))

    grad1, terms1 = layer_backward(grad_low, weights[1], seg, kept1)
    middle = (grad_low.astype(f32) + grad1).astype(bf16)
    grad0, terms0 = layer_backward(middle, weights[0], seg, kept0)
    first = middle.astype(f32) + grad0
    got = lax.ppermute(jnp.where(is_first, middle, first.astype(bf16)), "section", swap)
    got = got.astype(f32)
    own = jnp.where(is_first, first, middle.astype(f32))
    input_grads = jnp.where(is_first, jnp.stack([own, got]), jnp.stack([got, own]))

    def both(position):
        return jnp.stack([terms0[position], terms1[position]])

    def scatter(value, axis):
        return lax.psum_scatter(value, everyone, scatter_dimension=axis, tiled=True)

    grad_in = scatter(both(0).astype(bf16).reshape(2 * D, -1), 0).astype(f32)[None]
    grad_out = scatter(both(1).astype(bf16).reshape(2 * DI, -1), 0).astype(f32)[None]
    convg = both(3)
    packed = jnp.concatenate(
        [both(2).reshape(2, -1, nd),
         jnp.swapaxes(convg[:, :4].reshape(2, 4, -1, cut), 1, 2).reshape(2, -1, 4 * cut),
         convg[:, 4].reshape(2, -1, cut), both(4).reshape(2, -1, no)], -1
    )
    vec = scatter(packed.reshape(-1, packed.shape[-1]), 0)[0]
    head_sums = lax.psum(both(5)[:, :3], everyone)
    head_sums = jnp.where(is_first, head_sums[0], head_sums[1])
    return (
        section_outputs[None, :, None],
        input_grads[None, :, None],
        vec[None, :nd],
        grad_in,
        vec[nd : nd + 4 * cut].reshape(1, 4, cut),
        vec[None, nd + 4 * cut : nd + 5 * cut],
        head_sums[0:1],
        head_sums[1:2],
        head_sums[2:3],
        vec[None, nd + 5 * cut :],
        grad_out,
    )


def solution(mesh):
    placed = (
        P(None, "dp", "seq", None),
        P(None, "dp", "seq", None),
        P(None, "dp", "seq"),
        P("section", ("seq", "dp")),
        P("section", ("seq", "dp"), None),
        P("section", None, ("seq", "dp")),
        P("section", ("seq", "dp")),
        P("section", None),
        P("section", None),
        P("section", None),
        P("section", ("seq", "dp")),
        P("section", ("seq", "dp"), None),
    )
    return jax.shard_map(
        shards,
        mesh=mesh,
        in_specs=placed,
        out_specs=(
            P("section", None, "dp", "seq", None),
            P("section", None, "dp", "seq", None),
            P("section", ("seq", "dp")),
            P("section", ("seq", "dp"), None),
            P("section", None, ("seq", "dp")),
            P("section", ("seq", "dp")),
            P("section", None),
            P("section", None),
            P("section", None),
            P("section", ("seq", "dp")),
            P("section", ("seq", "dp"), None),
        ),
        check_vma=False,
    )
```

time: 1730 us -> 706 us (0.41)
  matrix products: 615 us -> 58.9 us
  other arithmetic: 304 us -> 35.5 us
  local copies, waits for them, and re-layouts: 281 us -> 49.7 us
  Pallas kernels: 0 us -> 91.3 us
  blocking collectives: 133 us -> 80.1 us
  waiting for transfers between devices: 313 us -> 342 us
    dot_general x62 -> x12, matrix products: 615 us -> 58.9 us  [dot(): lax.dot_general(a, b, (contract, ((), ())), precision=precision, preferre...]
    unnamed x13 -> x6, waiting for transfers between devices: 204 us -> 4.09 us
    reduce_scatter x1 -> x2, waiting for transfers between devices: 78.6 us -> 245 us  [scatter(): return lax.psum_scatter(value, everyone, scatter_dimension=axis, tiled=True)]
    slice x41 -> x17, local copies, waits for them, and re-layouts: 99.1 us -> 6.14 us  [the longest x1 1.28 us: shards(): vec[None, nd + 4 * cut:nd + 5 * cut]]
    pallas_call x0 -> x12, Pallas kernels: none -> 91.3 us  [the longest x2 36.3 us: layer_backward(): call(sweep_kernel, nc, [rc(DI), rc(2 * N), rc(H), rc(DI), rc(DI), rc(DI),...]
    reduce_sum x34 -> x1, other arithmetic: 88.9 us -> 1.37 us  [rms_scale(): jnp.mean(values * values, -1, keepdims=True) + EPS]
    mul x30 -> x0, other arithmetic: 77.7 us -> none  [the longest x5 39.4 us: conv_part(): activated = jax.nn.silu(conv_out)]
    all_gather x2, waiting for transfers between devices: 0.02 us -> 64.5 us  [the longest x1 36.9 us: shards(): lax.all_gather(in_weight, everyone, axis=1, tiled=True).reshape(2, D, -1)]
  transfers between devices with their start and end apart: 27 -> 17, of which waited for: 6 -> 10; matrix products, arithmetic and copies ran while one was open for 49% -> 13% of each run, Pallas kernels for 0% -> 4%
where the time goes in v1:
time: 706 us; the launch traced here: 697 us
  waiting for transfers between devices  342 us (48%)
  Pallas kernels  91.3 us (13%)
  blocking collectives  80.1 us (11%)
  matrix products  58.9 us (8%)
  local copies, waits for them, and re-layouts  49.7 us (7%)
  other arithmetic  35.5 us (5%)
  starting transfers between devices  23.8 us (3%)
  between operations  15.2 us (2%)
    reduce_scatter x2, waiting for transfers between devices, scatter(): return lax.psum_scatter(value, everyone, scatter_dimension=axis, tiled=True)  245 us
    dot_general x12, matrix products, dot(): lax.dot_general(a, b, (contract, ((), ())), precision=precision, preferre...  58.9 us
    unnamed x1, blocking collectives  40.6 us
    psum x1, blocking collectives, shards(): head_sums = lax.psum(both(5)[:, :3], everyone)  39.5 us
    all_gather x1, waiting for transfers between devices, shards(): lax.all_gather(in_weight, everyone, axis=1, tiled=True).reshape(2, D, -1)  36.9 us
    pallas_call x2, Pallas kernels, layer_backward(): call(sweep_kernel, nc, [rc(DI), rc(2 * N), rc(H), rc(DI), rc(DI), rc(DI),...  36.3 us
    all_gather x1, waiting for transfers between devices, shards(): lax.all_gather(out_weight, everyone, axis=1, tiled=True).reshape(2, DI, D)  27.6 us
    unnamed x130, local copies, waits for them, and re-layouts  26.1 us
  transfers between devices with their start and end apart: 17, of which 10 were waited for; matrix products, arithmetic and copies ran while one was open for 13% of the time, Pallas kernels for 4%

profile of v1, /device:TPU:0, one launch (start us, length us, event | category | flops | bytes accessed | tf_op | source)
XLA Modules:
  0.0 696.9 jit_solution(11230772865718125422)
XLA Ops:
  17.7 40.6 %all-reduce.4 = bf16[22528]{0:T(1024)(128)(2,1)S(1)} all-reduce(bf16[22528]{0:T(1024)(128)(2,1)S(1)} %dynamic-update-slice), channel_id=2, replica_groups=mesh['section'=2,'seq'=2,'dp'=8] {'section','seq','dp'}, use_global_device_ids=true, to_apply=%add.4 | all-reduce | flops 22528 | bytes 90112
  64.3 36.9 %all-gather.4.cloned.1.call-done = bf16[1,1536,3352]{2,1,0:T(8,128)(2,1)} async-done(((bf16[1,48,3352]{2,1,0:T(8,128)(2,1)}), bf16[1,1536,3352]{2,1,0:T(8,128)(2,1)}) %all-gather.4.cloned.1.call-update) | async-done | bytes 10297360 | tf_op jit(solution)/shard_map/all_gather | solution.py:546
  101.2 5.3 fusion.3.proj.z_ref.before
  112.5 3.0 copy-done.1
  115.5 6.8 shard_map.203
  129.4 5.4 shard_map.205
  138.8 27.6 %all-gather.6.cloned.1.call-done = bf16[1,3072,768]{2,1,0:T(8,128)(2,1)} async-done(((bf16[1,96,768]{2,1,0:T(8,128)(2,1)}), bf16[1,3072,768]{2,1,0:T(8,128)(2,1)}) %all-gather.6.cloned.1.call-update) | async-done | bytes 4718608 | tf_op jit(solution)/shard_map/all_gather | solution.py:547
  166.4 3.8 fusion.33
  170.2 5.6 fusion.5.proj.z_ref.before
  178.9 6.9 shard_map.206
  188.1 3.1 fusion.10.gno
  195.9 5.4 shard_map.208
  202.4 6.1 shard_map.209
  212.2 6.0 shard_map.210
  219.6 18.2 %shard_map.211 = (bf16[512,3352]{1,0:T(8,128)(2,1)}, f32[8,1792]{1,0:T(8,128)S(1)}, f32[8,24]{1,0:T(8,128)S(1)}, f32[8,1792]{1,0:T(8,128)S(1)}) custom-call(f32[512,1536]{1,0:T(8,128)S(1)} %get-tuple-element.77.dxi, f32[512,256]{1,0:T(8,128)S(1)} %get-tuple-element.78.dbc, f32[512,24]{1,0:T(8,128)S(1)} %get-tuple-element.79.dcum, ...), custom_call_target="tpu_custom_call" | custom-call | flops 4000000000 | bytes 20000000 | tf_op jit(solution)/shard_map/pallas_call | solution.py:469
  242.2 7.7 %fusion.22 = (f32[768]{0:T(1024)}, f32[512]{0:T(512)S(1)}, f32[512,768]{1,0:T(8,128)S(1)}) fusion(bf16[512,768]{1,0:T(8,128)(2,1)S(1)} %get-tuple-element.132, f32[512]{0:T(512)S(1)} %fusion.63, f32[768]{0:T(1024)S(1)} %mul.139, bf16[512,3352]{1,0:T(8,128)(2,1)S(1)} %fusion.52, bf16[1,1536,3352]{2,1,0:T(8,128)(2,1)} %all-gather.4.cloned.1.call-done), kind=kOutput, calls=%fused_computation.44 | convolution fusion | flops 2638871296 | bytes 11110400 | tf_op jit(solution)/shard_map/dot_general | solution.py:24
  252.6 6.7 shard_map.212
  262.0 5.9 shard_map.213
  270.7 4.6 fusion.6
  276.0 18.1 %shard_map.214 = (bf16[512,3352]{1,0:T(8,128)(2,1)}, f32[8,1792]{1,0:T(8,128)S(1)}, f32[8,24]{1,0:T(8,128)S(1)}, f32[8,1792]{1,0:T(8,128)S(1)}) custom-call(f32[512,1536]{1,0:T(8,128)S(1)} %copy-done.4, f32[512,256]{1,0:T(8,128)S(1)} %copy-done.24, f32[512,24]{1,0:T(8,128)S(1)} %get-tuple-element.90.dcum, bf16[512,1536]{1,0:T(8,128)(2,1)S(1)} %copy-done.14, ...), custom_call_target="tpu_custom_call" | custom-call | flops 4000000000 | bytes 20000000 | tf_op jit(solution)/shard_map/pallas_call | solution.py:469
  299.6 7.0 %fusion.23 = (f32[768]{0:T(1024)S(1)}, f32[512]{0:T(512)S(1)}, f32[512,768]{1,0:T(8,128)S(1)}) fusion(f32[512]{0:T(512)} %copy-done.46, bf16[2,1,512,768]{3,2,1,0:T(8,128)(2,1)} %param.12, s32[]{:T(128)S(6)} %select_n.101, f32[768]{0:T(1024)S(1)} %mul.133, bf16[512,3352]{1,0:T(8,128)(2,1)} %fusion.53, bf16[1,1536,3352]{2,1,0:T(8,128)(2,1)} %all-gather.4.cloned.1.call-done), kind=kOutput, calls=%fused_computation.45 | convolution fusion | flops 2638871296 | bytes 11216900 | tf_op jit(solution)/shard_map/dot_general | solution.py:24
  307.5 4.9 pad_maximum_fusion.1
  313.1 7.6 %fusion.1 = bf16[1,768,3352]{1,2,0:T(8,128)(2,1)} fusion(bf16[512,3352]{1,0:T(8,128)(2,1)} %copy-done.60, bf16[512,768]{1,0:T(8,128)(2,1)} %copy-done.44, f32[768]{0:T(1024)S(1)} %copy-done.52, f32[512]{0:T(512)S(1)} %copy-done.54), kind=kOutput, calls=%fused_computation.4 | convolution fusion | flops 2640267264 | bytes 9372672 | tf_op jit(solution)/shard_map/dot_general | solution.py:24
  320.7 5.3 fusion
  326.0 8.8 %pad_maximum_fusion = bf16[2,768,3352]{1,2,0:T(8,128)(2,1)} fusion(bf16[1,768,3352]{1,2,0:T(8,128)(2,1)} %fusion.1, bf16[1,768,3352]{1,2,0:T(8,128)(2,1)} %fusion), kind=kLoop, calls=%fused_computation | loop fusion | flops 5148672 | bytes 20594688 | tf_op jit(solution)/shard_map/stack | solution.py:585
  334.8 13.8 %copy.95 = bf16[2,768,3352]{2,1,0:T(8,128)(2,1)} copy(bf16[2,768,3352]{1,2,0:T(8,128)(2,1)} %pad_maximum_fusion) | data formatting | bytes 20594688 | tf_op jit(solution)/shard_map/stack | solution.py:585
  350.0 4.7 select_bitcast_fusion
  356.1 18.5 %collective-permute-done.6 = bf16[512,768]{1,0:T(8,128)(2,1)S(1)} collective-permute-done((bf16[512,768]{1,0:T(8,128)(2,1)}, bf16[512,768]{1,0:T(8,128)(2,1)S(1)}, u32[]{:S(2)}, u32[]{:S(2)}) %collective-permute-start.6) | collective-permute-done | bytes 786464 | tf_op jit(solution)/shard_map/ppermute | solution.py:571
  377.5 39.5 %psum.7 = f32[2,3,24]{2,1,0:T(4,128)S(1)} all-reduce(f32[2,3,24]{2,1,0:T(4,128)S(1)} %pad_maximum_fusion.6), channel_id=1, replica_groups=mesh['section'=2,'seq'=2,'dp'=8] {'section','seq','dp'}, use_global_device_ids=true, to_apply=%region_8.9 | all-reduce | flops 144 | bytes 1152 | tf_op jit(solution)/shard_map/psum | solution.py:599
  432.1 6.9 collective-permute-done.11
  441.0 99.1 %reduce-scatter.5.cloned.1.call-done = bf16[96,768]{1,0:T(8,128)(2,1)} async-done(((bf16[3072,768]{1,0:T(8,128)(2,1)}), bf16[96,768]{1,0:T(8,128)(2,1)}) %reduce-scatter.5.cloned.1.call-update) | async-done | bytes 147472 | tf_op jit(solution)/shard_map/reduce_scatter | solution.py:588
  541.7 146.4 %reduce-scatter.3.cloned.1.call-done = bf16[48,3352]{1,0:T(8,128)(2,1)} async-done(((bf16[1536,3352]{1,0:T(8,128)(2,1)}), bf16[48,3352]{1,0:T(8,128)(2,1)}) %reduce-scatter.3.cloned.1.call-update) | async-done | bytes 321808 | tf_op jit(solution)/shard_map/reduce_scatter | solution.py:588
  (261 shorter events, 95.8 us)
Async XLA Ops:
  7.2 53.9 %copy-start.50 = (s32[2,1,512]{2,1,0:T(1,128)S(1)}, s32[2,1,512]{2,1,0:T(1,128)}, u32[]{:S(2)}) copy-start(s32[2,1,512]{2,1,0:T(1,128)} %param.14) | copy-start | bytes 12292
  7.2 57.0 %copy-start.57 = (f32[1,24]{1,0:T(1,128)S(1)}, f32[1,24]{1,0:T(1,128)}, u32[]{:S(2)}) copy-start(f32[1,24]{1,0:T(1,128)} %param.19) | copy-start | bytes 292
  7.2 57.0 %copy-start.56 = (f32[1,24]{1,0:T(1,128)S(1)}, f32[1,24]{1,0:T(1,128)}, u32[]{:S(2)}) copy-start(f32[1,24]{1,0:T(1,128)} %param.21) | copy-start | bytes 292
  7.2 94.0 %copy-start.41 = (bf16[2,1,512,768]{3,2,1,0:T(8,128)(2,1)S(1)}, bf16[2,1,512,768]{3,2,1,0:T(8,128)(2,1)}, u32[]{:S(2)}) copy-start(bf16[2,1,512,768]{3,2,1,0:T(8,128)(2,1)} %param.12) | copy-start | bytes 4718596
  7.2 94.0 %all-gather.4.cloned.1.call-start = ((), (), s32[]{:S(2)}) async-start(), calls=%async_computation.2 | async-start | bytes 10948608 | tf_op jit(solution)/shard_map/all_gather | solution.py:546
  8.0 158.4 %all-gather.6.cloned.1.call-start = ((), (), s32[]{:S(2)}) async-start(), calls=%async_computation.3 | async-start | bytes 4866048 | tf_op jit(solution)/shard_map/all_gather | solution.py:547
  8.7 418.2 %all-reduce.8.cloned.1.call-start = ((), (), s32[]{:S(2)}) async-start(), calls=%async_computation.6 | async-start | bytes 196608
  9.5 52.9 %collective-permute-start.1 = (f32[3]{0:T(128)S(1)}, f32[3]{0:T(128)S(1)}, u32[]{:S(2)}, u32[]{:S(2)}) collective-permute-start(f32[3]{0:T(128)S(1)} %slice_bitcast_fusion.16), channel_id=1, source_target_pairs={{0,8},{1,9},{2,10},{3,11},{4,12},{5,13},{6,14},{7,15},{16,24},{17,... | collective-permute-start | bytes 44 | tf_op jit(solution)/shard_map/ppermute | solution.py:373
  13.2 51.0 %collective-permute-start.2 = (f32[3,24]{1,0:T(4,128)S(1)}, f32[3,24]{1,0:T(4,128)S(1)}, u32[]{:S(2)}, u32[]{:S(2)}) collective-permute-start(f32[3,24]{1,0:T(4,128)S(1)} %pad_maximum_fusion.9), channel_id=1, source_target_pairs={{0,16},{16,0},{1,17},{17,1},{2,18},{18,2},{3,19},{19,3},{4,20},{20... | collective-permute-start | bytes 872 | tf_op jit(solution)/shard_map/ppermute | solution.py:545
  59.7 190.2 %copy-start.51 = (f32[768]{0:T(1024)}, f32[768]{0:T(1024)S(1)}, u32[]{:S(2)}) copy-start(f32[768]{0:T(1024)S(1)} %mul.139) | copy-start | bytes 9220
  61.7 44.8 %copy-start.46 = (f32[512]{0:T(512)}, f32[512]{0:T(512)S(1)}, u32[]{:S(2)}) copy-start(f32[512]{0:T(512)S(1)} %fusion.62) | copy-start | bytes 6148
  62.4 50.1 %copy-start.25 = (f32[8,1792]{1,0:T(8,128)}, f32[8,1792]{1,0:T(8,128)S(1)}, u32[]{:S(2)}) copy-start(f32[8,1792]{1,0:T(8,128)S(1)} %get-tuple-element.130.convp) | copy-start | bytes 172036
  109.5 3.0 collective-permute-start
  122.3 7.1 %collective-permute-start.3 = (f32[128,1536]{1,0:T(8,128)S(1)}, f32[128,1536]{1,0:T(8,128)S(1)}, u32[]{:S(2)}, u32[]{:S(2)}) collective-permute-start(f32[128,1536]{1,0:T(8,128)S(1)} %get-tuple-element.64), channel_id=1, source_target_pairs={{0,8},{1,9},{2,10},{3,11},{4,12},{5,13},{6,14},{7,15},{16,24},{17,... | collective-permute-start | bytes 2359304 | tf_op jit(solution)/shard_map/ppermute | solution.py:373
  170.2 79.7 %copy-start.44 = (bf16[512,768]{1,0:T(8,128)(2,1)}, bf16[512,768]{1,0:T(8,128)(2,1)S(1)}, u32[]{:S(2)}) copy-start(bf16[512,768]{1,0:T(8,128)(2,1)S(1)} %get-tuple-element.132) | copy-start | bytes 2359300
  170.2 79.7 %copy-start.53 = (f32[512]{0:T(512)}, f32[512]{0:T(512)S(1)}, u32[]{:S(2)}) copy-start(f32[512]{0:T(512)S(1)} %fusion.63) | copy-start | bytes 6148
  175.8 3.1 collective-permute-start.4
  185.8 26.4 %copy-start.11 = (bf16[512,1536]{1,0:T(8,128)(2,1)}, bf16[512,1536]{1,0:T(8,128)(2,1)S(1)}, u32[]{:S(2)}) copy-start(bf16[512,1536]{1,0:T(8,128)(2,1)S(1)} %get-tuple-element.66.xt) | copy-start | bytes 4718596
  185.8 10.1 %collective-permute-start.5 = (f32[128,1536]{1,0:T(8,128)S(1)}, f32[128,1536]{1,0:T(8,128)S(1)}, u32[]{:S(2)}, u32[]{:S(2)}) collective-permute-start(f32[128,1536]{1,0:T(8,128)S(1)} %get-tuple-element.73), channel_id=1, source_target_pairs={{0,8},{1,9},{2,10},{3,11},{4,12},{5,13},{6,14},{7,15},{16,24},{17,... | collective-permute-start | bytes 2359304 | tf_op jit(solution)/shard_map/ppermute | solution.py:373
  210.9 7.3 %collective-permute-start.7 = (f32[128,1536]{1,0:T(8,128)S(1)}, f32[128,1536]{1,0:T(8,128)S(1)}, u32[]{:S(2)}, u32[]{:S(2)}) collective-permute-start(f32[128,1536]{1,0:T(8,128)S(1)} %get-tuple-element.83), channel_id=1, source_target_pairs={{8,0},{9,1},{10,2},{11,3},{12,4},{13,5},{14,6},{15,7},{24,16},{25,... | collective-permute-start | bytes 2359304 | tf_op jit(solution)/shard_map/ppermute | solution.py:373
  219.6 19.7 %copy-start.33 = (bf16[512,1536]{1,0:T(8,128)(2,1)S(1)}, bf16[512,1536]{1,0:T(8,128)(2,1)}, u32[]{:S(2)}) copy-start(bf16[512,1536]{1,0:T(8,128)(2,1)} %copy-done.32) | copy-start | bytes 4718596
  237.8 4.3 collective-permute-start.8
  260.5 14.7 %collective-permute-start.9 = (f32[128,1536]{1,0:T(8,128)}, f32[128,1536]{1,0:T(8,128)}, u32[]{:S(2)}, u32[]{:S(2)}) collective-permute-start(f32[128,1536]{1,0:T(8,128)} %get-tuple-element.94), channel_id=1, source_target_pairs={{8,0},{9,1},{10,2},{11,3},{12,4},{13,5},{14,6},{15,7},{24,16},{25,... | collective-permute-start | bytes 2359304 | tf_op jit(solution)/shard_map/ppermute | solution.py:373
  276.0 19.4 %copy-start.31 = (f32[8,1792]{1,0:T(8,128)S(1)}, f32[8,1792]{1,0:T(8,128)}, u32[]{:S(2)}) copy-start(f32[8,1792]{1,0:T(8,128)} %copy-done.30) | copy-start | bytes 172036
  294.1 4.0 collective-permute-start.10
  307.4 232.7 %reduce-scatter.5.cloned.1.call-start = ((), (), s32[]{:S(2)}) async-start(), calls=%async_computation.5 | async-start | bytes 4866048 | tf_op jit(solution)/shard_map/reduce_scatter | solution.py:588
  312.5 375.6 %reduce-scatter.3.cloned.1.call-start = ((), (), s32[]{:S(2)}) async-start(), calls=%async_computation.4 | async-start | bytes 10948608 | tf_op jit(solution)/shard_map/reduce_scatter | solution.py:588
  354.7 20.0 %collective-permute-start.6 = (bf16[512,768]{1,0:T(8,128)(2,1)}, bf16[512,768]{1,0:T(8,128)(2,1)S(1)}, u32[]{:S(2)}, u32[]{:S(2)}) collective-permute-start(bf16[512,768]{1,0:T(8,128)(2,1)} %get-tuple-element.108), channel_id=1, source_target_pairs={{0,16},{16,0},{1,17},{17,1},{2,18},{18,2},{3,19},{19,3},{4,20},{20... | collective-permute-start | bytes 2359304 | tf_op jit(solution)/shard_map/ppermute | solution.py:571
  374.7 42.3 %copy-start.49 = (f32[512]{0:T(512)S(1)}, f32[512]{0:T(512)}, u32[]{:S(2)}) copy-start(f32[512]{0:T(512)} %copy-done.48) | copy-start | bytes 6148
  374.7 42.4 %copy-start.39 = (bf16[512,768]{1,0:T(8,128)(2,1)S(1)}, bf16[512,768]{1,0:T(8,128)(2,1)}, u32[]{:S(2)}) copy-start(bf16[512,768]{1,0:T(8,128)(2,1)} %copy-done.38) | copy-start | bytes 2359300
  419.7 19.3 %collective-permute-start.11 = (bf16[512,768]{1,0:T(8,128)(2,1)}, bf16[512,768]{1,0:T(8,128)(2,1)S(1)}, u32[]{:S(2)}, u32[]{:S(2)}) collective-permute-start(bf16[512,768]{1,0:T(8,128)(2,1)} %convert_select_fusion.1), channel_id=1, source_target_pairs={{0,16},{16,0},{1,17},{17,1},{2,18},{18,2},{3,19},{19,3},{4,20},{20... | collective-permute-start | bytes 2359304 | tf_op jit(solution)/shard_map/ppermute | solution.py:579
  424.3 14.9 %copy-start.40 = (f32[1,1,1,512,768]{4,3,2,1,0:T(8,128)S(1)}, f32[1,1,1,512,768]{4,3,2,1,0:T(8,128)}, u32[]{:S(2)}) copy-start(f32[1,1,1,512,768]{4,3,2,1,0:T(8,128)} %fusion.25) | copy-start | bytes 4718596
  (48 other events, 227.9 us)
Sparse Core Ops, SparseCore 0:
  11.0 90.1 all-gather.3
  104.1 62.2 all-gather.5
  307.5 119.3 all-reduce.7
  432.2 107.7 reduce-scatter.4
  547.1 140.9 reduce-scatter.2
